TPU v7x, 32 devices: a whole 2x2x4 slice. The times are simulated.
32 devices in a mesh: sub: 8 (over z, y), freq: 4 (over x, core).
Axes of the slice: x: 2, y: 2, z: 4, core: 2. Of those that a mesh axis runs over, the one named last changes fastest.
Arguments:
- response: bfloat16 [4, 96, 96, 256], P('freq', 'sub'), may hold values from -6 to 6
- measured: bfloat16 [4, 768, 256], P('freq', 'sub'), may hold values from -6 to 6
- sensor_owner: int32 [768], P('sub'), may hold values from 0 to 7, as said below
- sensor_row: int32 [768], P('sub'), may hold values from 0 to 1151
- adj_diag: bfloat16 [4, 96, 2, 96, 96], P('freq', 'sub')
- adj_off: bfloat16 [4, 96, 5, 2, 96, 96], P('freq', 'sub')
- block_cols: int32 [96, 5], P('sub'), may hold values from 0 to 13, as said below
- precond: bfloat16 [4, 96, 2, 96, 96], P('freq', 'sub')
- stiff_deriv: bfloat16 [96, 96, 96], P('sub'), may hold values from -0.625 to 0.625
Outputs:
- adjoint: bfloat16 [4, 96, 96, 256], P('freq', 'sub')
- gradient: float32 [96], P('sub')
Inputs may be any that keep to these rules, and one draw needn't show every extreme that they name: `sensor_owner`: among the 96 channels held by one index of sub, no subdomain is named more than 36 times, and one subdomain is named exactly 36 times by the channels of every index of sub. `block_cols`: in every subdomain some block row has a coupling tile with column 0 and some has one with column 13.
All inputs are finite; a program needn't handle non-finite values.
Results may differ from a plain program's by a relative error of at most 0.0061.
Values may be sent and summed in bfloat16 or wider, within the bound.
A program may use at most 64 MiB of HBM per device.

v0:
```python
import math

import jax
import jax.numpy as jnp
from jax import lax
from jax.sharding import PartitionSpec as P

SWEEPS = 3


def with_halo(block, sides, width):
    for axis, dim in sides:
        count = lax.axis_size(axis)
        forward = [(i, i + 1) for i in range(count - 1)]
        backward = [(target, source) for source, target in forward]
        low = lax.ppermute(
            lax.slice_in_dim(block, block.shape[dim] - width, None, axis=dim), axis, forward
        )
        high = lax.ppermute(lax.slice_in_dim(block, 0, width, axis=dim), axis, backward)
        block = jnp.concatenate([low, block, high], axis=dim)
    return block


def complex_apply(tile_set, vectors):
    column_half = vectors.shape[-1] // 2
    real_part = jnp.einsum(
        "bij,bjn->bin", tile_set[:, 0], vectors, preferred_element_type=jnp.float32
    )
    imag_part = jnp.einsum(
        "bij,bjn->bin", tile_set[:, 1], vectors, preferred_element_type=jnp.float32
    )
    return jnp.concatenate(
        [
            real_part[..., :column_half] - imag_part[..., column_half:],
            real_part[..., column_half:] + imag_part[..., :column_half],
        ],
        axis=-1,
    )


def coupled_apply(tile_set, gathered):
    column_half = gathered.shape[-1] // 2
    real_part = jnp.einsum(
        "bkij,bkjn->bin", tile_set[:, :, 0], gathered, preferred_element_type=jnp.float32
    )
    imag_part = jnp.einsum(
        "bkij,bkjn->bin", tile_set[:, :, 1], gathered, preferred_element_type=jnp.float32
    )
    return jnp.concatenate(
        [
            real_part[..., :column_half] - imag_part[..., column_half:],
            real_part[..., column_half:] + imag_part[..., :column_half],
        ],
        axis=-1,
    )


def shards(
    response,
    measured,
    sensor_owner,
    sensor_row,
    adj_diag,
    adj_off,
    block_cols,
    precond,
    stiff_deriv,
):
    own_resp = response[0]
    block_count, rows_per, col_count = own_resp.shape
    flat_resp = own_resp.reshape(block_count * rows_per, col_count)
    local_measurements = measured[0]
    my_index = lax.axis_index("sub")
    empty_load = jnp.zeros((block_count * rows_per, col_count), jnp.float32)
    incoming_rows = lax.all_gather(local_measurements, "sub", axis=0, tiled=True)
    owners_in = lax.all_gather(sensor_owner, "sub", axis=0, tiled=True)
    index_in = lax.all_gather(sensor_row, "sub", axis=0, tiled=True)
    owned = owners_in == my_index
    safe_index = jnp.where(owned, index_in, 0)
    predicted = flat_resp[safe_index].astype(jnp.float32)
    misfit = jnp.where(owned[:, None], predicted - incoming_rows.astype(jnp.float32), 0.0)
    load_flat = empty_load.at[safe_index].add(misfit)
    load_rhs = load_flat.reshape(block_count, rows_per, col_count)
    diag_tiles = adj_diag[0]
    off_tiles = adj_off[0]
    prec_tiles = precond[0]
    adjoint = complex_apply(prec_tiles, load_rhs.astype(jnp.bfloat16))
    for jacobi_sweep_step in range(SWEEPS - 1):
        iterate = adjoint.astype(jnp.bfloat16)
        extended = with_halo(iterate, (("sub", 0),), 1)
        gathered = extended[block_cols]
        applied = complex_apply(diag_tiles, iterate) + coupled_apply(off_tiles, gathered)
        update = (load_rhs - applied).astype(jnp.bfloat16)
        adjoint = adjoint + complex_apply(prec_tiles, update)
    stiff_resp = jnp.einsum(
        "bij,bjn->bin", stiff_deriv, own_resp, preferred_element_type=jnp.float32
    )
    grad_scale = 1.0 / math.sqrt(rows_per * col_count)
    partial_grad = jnp.sum(adjoint * stiff_resp, axis=(1, 2)) * grad_scale
    gradient = lax.psum(partial_grad, "freq")
    return (adjoint.astype(jnp.bfloat16)[None], gradient)


def solution(mesh):
    in_specs = (
        P("freq", "sub", None, None),
        P("freq", "sub", None),
        P("sub"),
        P("sub"),
        P("freq", "sub", None, None, None),
        P("freq", "sub", None, None, None, None),
        P("sub", None),
        P("freq", "sub", None, None, None),
        P("sub", None, None),
    )
    out_specs = (P("freq", "sub", None, None), P("sub"))
    return jax.shard_map(shards, mesh=mesh, in_specs=in_specs, out_specs=out_specs, check_vma=False)
```

profile of v0, /device:TPU:0, one launch (start us, length us, event | category | flops | bytes accessed | tf_op | source)
XLA Modules:
  0.0 118.8 jit_solution(1274034666612511459)
XLA Ops:
  0.6 1.3 %dynamic-slice = u32[1]{0:T(128)} dynamic-slice(u32[32]{0:T(128)} %constant.28, u32[]{:T(128)S(6)} %add.78), dynamic_slice_sizes={1} | dynamic-slice | bytes 12
  4.3 13.2 %all-reduce.2 = (s32[768]{0:T(1024)S(1)}, s32[768]{0:T(1024)S(1)}) all-reduce(s32[768]{0:T(1024)S(1)} %dynamic-update-slice, s32[768]{0:T(1024)S(1)} %dynamic-update-slice.1), channel_id=1, replica_groups=mesh['sub'=8,'freq'=4] {'sub'}, use_global_device_ids=true, to_apply=%add | all-reduce | flops 1536 | bytes 12288
  17.5 31.4 %all-gather = bf16[1,768,256]{2,1,0:T(8,128)(2,1)S(1)} all-gather(bf16[1,96,256]{2,1,0:T(8,128)(2,1)} %param.10), channel_id=2, replica_groups=mesh['sub'=8,'freq'=4] {'sub'}, dimensions={1}, use_global_device_ids=true | all-gather | bytes 442368 | tf_op jit(solution)/shard_map/all_gather | solution.py:75
  48.9 1.1 copy.28
  50.0 10.9 %scatter_custom_fusion = f32[1152,256]{1,0:T(8,128)S(1)} fusion(s32[768]{0:T(1024)S(1)} %get-tuple-element.4, f32[]{:T(128)} %constant.7.clone.1, bf16[1,768,256]{2,1,0:T(8,128)(2,1)S(1)} %all-gather, pred[768]{0:T(1024)(128)(4,1)S(1)} %get-tuple-element.5, bf16[1152,256]{1,0:T(8,128)(2,1)S(1)} %bitcast.108, s32[1024]{0:T(1024)S(1)} %pad_clamp_fusion.1), kind=kCustom, calls=%fused_computation.38 | custom fusion | flops 983040 | bytes 2168832 | tf_op jit(solution)/shard_map/scatter-add | solution.py:82
  62.5 1.9 %collective-permute-start = (bf16[1,96,256]{2,1,0:T(8,128)(2,1)}, bf16[1,96,256]{2,1,0:T(8,128)(2,1)}, u32[]{:S(2)}, u32[]{:S(2)}) collective-permute-start(bf16[1,96,256]{2,1,0:T(8,128)(2,1)} %get-tuple-element.22), channel_id=1, source_target_pairs={{0,4},{4,8},{8,12},{12,16},{16,20},{20,24},{24,28},{1,5},{5,9},{9,... | collective-permute-start | bytes 147464 | tf_op jit(solution)/shard_map/ppermute | solution.py:16
  64.4 1.3 %collective-permute-start.1 = (bf16[1,96,256]{2,1,0:T(8,128)(2,1)}, bf16[1,96,256]{2,1,0:T(8,128)(2,1)}, u32[]{:S(2)}, u32[]{:S(2)}) collective-permute-start(bf16[1,96,256]{2,1,0:T(8,128)(2,1)} %get-tuple-element.23), channel_id=1, source_target_pairs={{4,0},{8,4},{12,8},{16,12},{20,16},{24,20},{28,24},{5,1},{9,5},{13... | collective-permute-start | bytes 147464 | tf_op jit(solution)/shard_map/ppermute | solution.py:19
  66.1 1.3 %convolution_bitcast_fusion.10 = f32[12,96,256]{2,1,0:T(8,128)} fusion(bf16[12,96,256]{2,1,0:T(8,128)(2,1)S(1)} %fusion.7, bf16[12,2,96,96]{3,2,0,1:T(8,128)(2,1)S(1)} %bitcast.134), kind=kOutput, calls=%fused_computation.18 | convolution fusion | flops 56623104 | bytes 2064384 | tf_op jit(solution)/shard_map/bij,bjn->bin/dot_general | solution.py:29
  67.6 2.6 %slice_subtract_fusion.5 = (f32[12,96,128]{2,1,0:T(8,128)}, f32[12,96,128]{2,1,0:T(8,128)}) fusion(f32[12,96,256]{2,1,0:T(8,128)} %convolution_bitcast_fusion.10, f32[12,96,256]{2,1,0:T(8,128)S(1)} %convolution_bitcast_fusion.11), kind=kLoop, calls=%fused_computation.53 | loop fusion | flops 294912 | bytes 3538944 | tf_op jit(solution)/shard_map/sub | solution.py:34
  70.2 1.8 %copy.26 = bf16[1,12,5,2,96,96]{5,4,2,1,3,0:T(8,128)(2,1)} copy(bf16[1,12,5,2,96,96]{5,4,3,2,1,0:T(8,128)(2,1)S(1)} %copy-done.18) | data formatting | bytes 4423680 | tf_op args[5]
  72.1 0.9 pad_maximum_fusion.1
  73.0 2.4 %gather_fusion = bf16[60,96,256]{2,1,0:T(8,128)(2,1)} fusion(bf16[14,96,256]{2,1,0:T(8,128)(2,1)S(1)} %pad_maximum_fusion.1, s32[1024]{0:T(1024)S(1)} %pad_clamp_fusion), kind=kCustom, calls=%fused_computation.1 | custom fusion | bytes 5898480 | tf_op jit(solution)/shard_map/gather | solution.py:91
  75.4 3.1 %convolution_bitcast_fusion.8 = f32[12,96,256]{2,1,0:T(8,128)S(1)} fusion(bf16[12,5,96,256]{3,2,1,0:T(8,128)(2,1)} %bitcast.119, bf16[12,5,2,96,96]{4,3,1,0,2:T(8,128)(2,1)} %bitcast.113), kind=kOutput, calls=%fused_computation.16 | convolution fusion | flops 283115520 | bytes 5603328 | tf_op jit(solution)/shard_map/bkij,bkjn->bin/dot_general | solution.py:46
  78.5 2.5 %convolution_bitcast_fusion.9 = f32[12,96,256]{2,1,0:T(8,128)S(1)} fusion(bf16[12,5,96,256]{3,2,1,0:T(8,128)(2,1)} %bitcast.120, bf16[12,5,2,96,96]{4,3,1,0,2:T(8,128)(2,1)S(1)} %bitcast.115), kind=kOutput, calls=%fused_computation.17 | convolution fusion | flops 283115520 | bytes 5603328 | tf_op jit(solution)/shard_map/bkij,bkjn->bin/dot_general | solution.py:43
  84.1 0.9 copy-done.4
  86.7 4.6 %collective-permute-start.2 = (bf16[1,96,256]{2,1,0:T(8,128)(2,1)S(1)}, bf16[1,96,256]{2,1,0:T(8,128)(2,1)S(1)}, u32[]{:S(2)}, u32[]{:S(2)}) collective-permute-start(bf16[1,96,256]{2,1,0:T(8,128)(2,1)S(1)} %get-tuple-element.20), channel_id=1, source_target_pairs={{0,4},{4,8},{8,12},{12,16},{16,20},{20,24},{24,28},{1,5},{5,9},{9,... | collective-permute-start | bytes 147464 | tf_op jit(solution)/shard_map/ppermute | solution.py:16
  91.3 1.5 %collective-permute-start.3 = (bf16[1,96,256]{2,1,0:T(8,128)(2,1)S(1)}, bf16[1,96,256]{2,1,0:T(8,128)(2,1)S(1)}, u32[]{:S(2)}, u32[]{:S(2)}) collective-permute-start(bf16[1,96,256]{2,1,0:T(8,128)(2,1)S(1)} %get-tuple-element.21), channel_id=1, source_target_pairs={{4,0},{8,4},{12,8},{16,12},{20,16},{24,20},{28,24},{5,1},{9,5},{13... | collective-permute-start | bytes 147464 | tf_op jit(solution)/shard_map/ppermute | solution.py:19
  92.8 1.2 %slice_subtract_fusion.2 = (f32[12,96,128]{2,1,0:T(8,128)}, f32[12,96,128]{2,1,0:T(8,128)}) fusion(f32[12,96,256]{2,1,0:T(8,128)S(1)} %convolution_bitcast_fusion.4, f32[12,96,256]{2,1,0:T(8,128)S(1)} %convolution_bitcast_fusion.5), kind=kLoop, calls=%fused_computation.47 | loop fusion | flops 294912 | bytes 3538944 | tf_op jit(solution)/shard_map/sub | solution.py:34
  94.0 3.3 %collective-permute-done.3 = bf16[1,96,256]{2,1,0:T(8,128)(2,1)S(1)} collective-permute-done((bf16[1,96,256]{2,1,0:T(8,128)(2,1)S(1)}, bf16[1,96,256]{2,1,0:T(8,128)(2,1)S(1)}, u32[]{:S(2)}, u32[]{:S(2)}) %collective-permute-start.3) | collective-permute-done | bytes 49184 | tf_op jit(solution)/shard_map/ppermute | solution.py:19
  97.4 2.4 %gather_fusion.1 = bf16[60,96,256]{2,1,0:T(8,128)(2,1)} fusion(bf16[14,96,256]{2,1,0:T(8,128)(2,1)S(1)} %pad_maximum_fusion.2, s32[1024]{0:T(1024)S(1)} %pad_clamp_fusion), kind=kCustom, calls=%fused_computation.2 | custom fusion | bytes 5898480 | tf_op jit(solution)/shard_map/gather | solution.py:91
  99.8 3.1 %convolution_bitcast_fusion.2 = f32[12,96,256]{2,1,0:T(8,128)S(1)} fusion(bf16[12,5,96,256]{3,2,1,0:T(8,128)(2,1)} %bitcast.117, bf16[12,5,2,96,96]{4,3,1,0,2:T(8,128)(2,1)} %bitcast.114), kind=kOutput, calls=%fused_computation.10 | convolution fusion | flops 283115520 | bytes 5603328 | tf_op jit(solution)/shard_map/bkij,bkjn->bin/dot_general | solution.py:46
  102.9 2.5 %convolution_bitcast_fusion.3 = f32[12,96,256]{2,1,0:T(8,128)S(1)} fusion(bf16[12,5,96,256]{3,2,1,0:T(8,128)(2,1)} %bitcast.118, bf16[12,5,2,96,96]{4,3,1,0,2:T(8,128)(2,1)S(1)} %bitcast.116), kind=kOutput, calls=%fused_computation.11 | convolution fusion | flops 283115520 | bytes 5603328 | tf_op jit(solution)/shard_map/bkij,bkjn->bin/dot_general | solution.py:43
  110.5 6.2 %psum.7 = f32[12]{0:T(128)} all-reduce(f32[12]{0:T(128)S(1)} %broadcast_multiply_fusion), channel_id=1, replica_groups=mesh['sub'=8,'freq'=4] {'freq'}, use_global_device_ids=true, to_apply=%region_2.3 | all-reduce | flops 12 | bytes 96 | tf_op jit(solution)/shard_map/psum | solution.py:100
  116.7 2.1 %fusion.2 = bf16[1,12,96,256]{3,2,1,0:T(8,128)(2,1)} fusion(f32[1,12,96,128]{3,2,1,0:T(8,128)S(1)} %bitcast.122, f32[1,12,96,128]{3,2,1,0:T(8,128)S(1)} %bitcast.121, f32[1,12,96,128]{3,2,1,0:T(8,128)S(1)} %bitcast.124, f32[1,12,96,128]{3,2,1,0:T(8,128)S(1)} %bitcast.123, f32[1,12,96,128]{3,2,1,0:T(8,128)} %bitcast.132, f32[1,12,96,128]{3,2,1,0:T(8,128)S(1)} %bitcast.131), kind=kLoop, calls=%fused_computation.25 | loop fusion | flops 1769472 | bytes 4128768 | tf_op jit(solution)/shard_map/convert_element_type | solution.py:101
  (88 shorter events, 13.6 us)
Async XLA Ops:
  0.6 49.4 %copy-start = (bf16[1,12,96,256]{3,2,1,0:T(8,128)(2,1)S(1)}, bf16[1,12,96,256]{3,2,1,0:T(8,128)(2,1)}, u32[]{:S(2)}) copy-start(bf16[1,12,96,256]{3,2,1,0:T(8,128)(2,1)} %param.9) | copy-start | bytes 1769476
  50.0 11.3 %copy-start.12 = (bf16[1,12,2,96,96]{4,3,1,2,0:T(8,128)(2,1)}, bf16[1,12,2,96,96]{4,3,1,2,0:T(8,128)(2,1)S(1)}, u32[]{:S(2)}) copy-start(bf16[1,12,2,96,96]{4,3,1,2,0:T(8,128)(2,1)S(1)} %copy.28) | copy-start | bytes 1327108
  61.7 4.0 %copy-start.3 = (f32[12,96,128]{2,1,0:T(8,128)}, f32[12,96,128]{2,1,0:T(8,128)S(1)}, u32[]{:S(2)}) copy-start(f32[12,96,128]{2,1,0:T(8,128)S(1)} %get-tuple-element.19) | copy-start | bytes 1769476
  61.7 3.9 %copy-start.23 = (bf16[1,12,2,96,96]{4,3,2,1,0:T(8,128)(2,1)S(1)}, bf16[1,12,2,96,96]{4,3,2,1,0:T(8,128)(2,1)}, u32[]{:S(2)}) copy-start(bf16[1,12,2,96,96]{4,3,2,1,0:T(8,128)(2,1)} %param.13) | copy-start | bytes 1327108
  61.8 4.2 %copy-start.6 = (bf16[12,96,256]{2,1,0:T(8,128)(2,1)}, bf16[12,96,256]{2,1,0:T(8,128)(2,1)S(1)}, u32[]{:S(2)}) copy-start(bf16[12,96,256]{2,1,0:T(8,128)(2,1)S(1)} %fusion.7) | copy-start | bytes 1769476
  62.5 9.6 %collective-permute-start = (bf16[1,96,256]{2,1,0:T(8,128)(2,1)}, bf16[1,96,256]{2,1,0:T(8,128)(2,1)}, u32[]{:S(2)}, u32[]{:S(2)}) collective-permute-start(bf16[1,96,256]{2,1,0:T(8,128)(2,1)} %get-tuple-element.22), channel_id=1, source_target_pairs={{0,4},{4,8},{8,12},{12,16},{16,20},{20,24},{24,28},{1,5},{5,9},{9,... | collective-permute-start | bytes 147464 | tf_op jit(solution)/shard_map/ppermute | solution.py:16
  64.4 7.7 %collective-permute-start.1 = (bf16[1,96,256]{2,1,0:T(8,128)(2,1)}, bf16[1,96,256]{2,1,0:T(8,128)(2,1)}, u32[]{:S(2)}, u32[]{:S(2)}) collective-permute-start(bf16[1,96,256]{2,1,0:T(8,128)(2,1)} %get-tuple-element.23), channel_id=1, source_target_pairs={{4,0},{8,4},{12,8},{16,12},{20,16},{24,20},{28,24},{5,1},{9,5},{13... | collective-permute-start | bytes 147464 | tf_op jit(solution)/shard_map/ppermute | solution.py:19
  65.7 1.7 %copy-start.16 = (bf16[1,12,2,96,96]{4,3,1,2,0:T(8,128)(2,1)}, bf16[1,12,2,96,96]{4,3,1,2,0:T(8,128)(2,1)S(1)}, u32[]{:S(2)}) copy-start(bf16[1,12,2,96,96]{4,3,1,2,0:T(8,128)(2,1)S(1)} %copy.27) | copy-start | bytes 1327108
  66.0 1.3 %copy-start.25 = (s32[12,5]{0,1:T(8,128)S(1)}, s32[12,5]{0,1:T(8,128)}, u32[]{:S(2)}) copy-start(s32[12,5]{0,1:T(8,128)} %param.15) | copy-start | bytes 724
  67.6 2.6 %copy-start.18 = (bf16[1,12,5,2,96,96]{5,4,3,2,1,0:T(8,128)(2,1)S(1)}, bf16[1,12,5,2,96,96]{5,4,3,2,1,0:T(8,128)(2,1)}, u32[]{:S(2)}) copy-start(bf16[1,12,5,2,96,96]{5,4,3,2,1,0:T(8,128)(2,1)} %param.14) | copy-start | bytes 6635524
  70.2 1.9 %copy-start.7 = (bf16[12,96,256]{2,1,0:T(8,128)(2,1)S(1)}, bf16[12,96,256]{2,1,0:T(8,128)(2,1)}, u32[]{:S(2)}) copy-start(bf16[12,96,256]{2,1,0:T(8,128)(2,1)} %copy-done.6) | copy-start | bytes 1769476
  75.4 3.2 %copy-start.1 = (bf16[1,12,5,2,96,96]{5,4,2,1,3,0:T(8,128)(2,1)S(1)}, bf16[1,12,5,2,96,96]{5,4,2,1,3,0:T(8,128)(2,1)}, u32[]{:S(2)}) copy-start(bf16[1,12,5,2,96,96]{5,4,2,1,3,0:T(8,128)(2,1)} %copy.26) | copy-start | bytes 6635524
  81.1 1.2 %copy-start.20 = (f32[12,96,128]{2,1,0:T(8,128)S(1)}, f32[12,96,128]{2,1,0:T(8,128)}, u32[]{:S(2)}) copy-start(f32[12,96,128]{2,1,0:T(8,128)} %get-tuple-element.17) | copy-start | bytes 1769476
  84.0 1.1 copy-start.4
  84.1 1.1 copy-start.8
  84.1 1.1 copy-start.10
  86.7 7.3 %collective-permute-start.2 = (bf16[1,96,256]{2,1,0:T(8,128)(2,1)S(1)}, bf16[1,96,256]{2,1,0:T(8,128)(2,1)S(1)}, u32[]{:S(2)}, u32[]{:S(2)}) collective-permute-start(bf16[1,96,256]{2,1,0:T(8,128)(2,1)S(1)} %get-tuple-element.20), channel_id=1, source_target_pairs={{0,4},{4,8},{8,12},{12,16},{16,20},{20,24},{24,28},{1,5},{5,9},{9,... | collective-permute-start | bytes 147464 | tf_op jit(solution)/shard_map/ppermute | solution.py:16
  91.3 6.0 %collective-permute-start.3 = (bf16[1,96,256]{2,1,0:T(8,128)(2,1)S(1)}, bf16[1,96,256]{2,1,0:T(8,128)(2,1)S(1)}, u32[]{:S(2)}, u32[]{:S(2)}) collective-permute-start(bf16[1,96,256]{2,1,0:T(8,128)(2,1)S(1)} %get-tuple-element.21), channel_id=1, source_target_pairs={{4,0},{8,4},{12,8},{16,12},{20,16},{24,20},{28,24},{5,1},{9,5},{13... | collective-permute-start | bytes 147464 | tf_op jit(solution)/shard_map/ppermute | solution.py:19
  99.8 3.2 %copy-start.2 = (bf16[1,12,5,2,96,96]{5,4,2,1,3,0:T(8,128)(2,1)S(1)}, bf16[1,12,5,2,96,96]{5,4,2,1,3,0:T(8,128)(2,1)}, u32[]{:S(2)}) copy-start(bf16[1,12,5,2,96,96]{5,4,2,1,3,0:T(8,128)(2,1)} %copy.26) | copy-start | bytes 6635524
  105.4 1.2 %copy-start.22 = (f32[12,96,128]{2,1,0:T(8,128)S(1)}, f32[12,96,128]{2,1,0:T(8,128)}, u32[]{:S(2)}) copy-start(f32[12,96,128]{2,1,0:T(8,128)} %get-tuple-element.11) | copy-start | bytes 1769476
  108.4 1.4 %copy-start.9 = (f32[12,96,128]{2,1,0:T(8,128)S(1)}, f32[12,96,128]{2,1,0:T(8,128)}, u32[]{:S(2)}) copy-start(f32[12,96,128]{2,1,0:T(8,128)} %copy-done.8) | copy-start | bytes 1769476
  108.4 1.6 %copy-start.11 = (f32[12,96,128]{2,1,0:T(8,128)S(1)}, f32[12,96,128]{2,1,0:T(8,128)}, u32[]{:S(2)}) copy-start(f32[12,96,128]{2,1,0:T(8,128)} %copy-done.10) | copy-start | bytes 1769476
  108.4 1.7 %copy-start.24 = (bf16[12,96,96]{2,1,0:T(8,128)(2,1)S(1)}, bf16[12,96,96]{2,1,0:T(8,128)(2,1)}, u32[]{:S(2)}) copy-start(bf16[12,96,96]{2,1,0:T(8,128)(2,1)} %param.17) | copy-start | bytes 663556
  108.5 2.0 %copy-start.15 = (f32[12,96,128]{2,1,0:T(8,128)}, f32[12,96,128]{2,1,0:T(8,128)S(1)}, u32[]{:S(2)}) copy-start(f32[12,96,128]{2,1,0:T(8,128)S(1)} %get-tuple-element.7) | copy-start | bytes 1769476
  (6 other events, 6.4 us)
where the time goes:
time: 119 us
  blocking collectives  50.7 us (43%)
  other arithmetic  19.5 us (16%)
  local copies, waits for them, and re-layouts  18.7 us (16%)
  matrix products  15.6 us (13%)
  starting transfers between devices  9.2 us (8%)
  waiting for transfers between devices  3.28 us (3%)
  between operations  1.73 us (1%)
    all_gather x1, blocking collectives, shards(): lax.all_gather(local_measurements, 'sub', axis=0, tiled=True)  31.4 us
    unnamed x1, blocking collectives  13.2 us
    unnamed x60, local copies, waits for them, and re-layouts  13.1 us
    scatter-add x1, other arithmetic, shards(): load_flat = empty_load.at[safe_index].add(misfit)  10.9 us
    ppermute x2, starting transfers between devices, with_halo(): lax.ppermute(lax.slice_in_dim(block, block.shape[dim] - width, None, axis...  6.45 us
    psum x1, blocking collectives, shards(): gradient = lax.psum(partial_grad, 'freq')  6.16 us
    dot_general x2, matrix products, coupled_apply(): jnp.einsum('bkij,bkjn->bin', tile_set[:, :, 1], gathered, preferred_eleme...  6.15 us
    dot_general x2, matrix products, coupled_apply(): jnp.einsum('bkij,bkjn->bin', tile_set[:, :, 0], gathered, preferred_eleme...  5.01 us
  transfers between devices with their start and end apart: 4, of which 1 were waited for; matrix products, arithmetic and copies ran while one was open for 6% of the time, Pallas kernels for 0%

commit v1 on v0

v1 whole, which is shorter than its diff:
```python
import functools
import math

import jax
import jax.numpy as jnp
from jax import lax
from jax.experimental import pallas as pl
from jax.experimental.pallas import tpu as pltpu
from jax.sharding import PartitionSpec as P

MESH = pl.DeviceIdType.MESH
F32 = jnp.float32
BF16 = jnp.bfloat16
SWEEPS = 3
LANES = 128
CAPS = {8: 36, 128: 3}


def round_up(value, unit):
    return -(-value // unit) * unit


def iota(shape, dim):
    return lax.broadcasted_iota(jnp.int32, shape, dim)


def one_hot(mask):
    return jnp.where(mask, 1.0, 0.0).astype(BF16)


def dot(a, b):
    return jnp.dot(a, b, preferred_element_type=F32)


def combine(prod):
    rows, half = prod.shape[0] // 2, prod.shape[1] // 2
    left = prod[:rows, :half] - prod[rows:, half:]
    right = prod[:rows, half:] + prod[rows:, :half]
    return jnp.concatenate([left, right], axis=1)


def kernel(
    n_sub, n_freq, slots, group,
    resp_hbm, meas, owner, row, diag_hbm, off_hbm, cols, prec_hbm, stiff_hbm,
    out, grad,
    resp, diag, off, prec, stiff, tiles, ext_0, ext_1, load, lam, stiff_resp, scat,
    idx_send, idx_recv, pack_send, pack_recv, meas_all, part, part_recv,
    in_sem, idx_ss, idx_rs, pack_ss, pack_rs, halo_ss, halo_rs, part_ss, part_rs,
):
    nb, bs, width = resp.shape
    nnb = off.shape[1]
    half = width // 2
    ext = (ext_0, ext_1)
    chans = meas.shape[0]
    lanes = scat.shape[2]
    me = lax.axis_index("sub")
    fr = lax.axis_index("freq")

    loads = [
        pltpu.make_async_copy(src, dst, in_sem.at[i])
        for i, (src, dst) in enumerate(
            [(resp_hbm, resp), (stiff_hbm, stiff), (diag_hbm, diag), (off_hbm, off), (prec_hbm, prec)]
        )
    ]
    for copy in loads:
        copy.start()

    barrier = pltpu.get_barrier_semaphore()
    for j in range(1, n_sub):
        pl.semaphore_signal(barrier, inc=1, device_id={"sub": lax.rem(me + j, n_sub)}, device_id_type=MESH)
    for j in range(1, n_freq):
        pl.semaphore_signal(barrier, inc=1, device_id={"freq": lax.rem(fr + j, n_freq)}, device_id_type=MESH)

    own = owner[...].astype(F32)
    ri, ci = iota((chans, chans), 0), iota((chans, chans), 1)
    own_b = jnp.broadcast_to(own, (chans, chans))
    own_col = jnp.sum(jnp.where(ri == ci, own_b, 0.0), axis=1, keepdims=True)
    same = jnp.where(own_col == own_b, 1.0, 0.0)
    rank = jnp.sum(jnp.where(ri < ci, same, 0.0), axis=0, keepdims=True)
    rank_col = jnp.sum(jnp.where(ci < ri, same, 0.0), axis=1, keepdims=True)
    number = row[...].astype(F32) + 1.0
    high = jnp.floor(number * (1.0 / 64.0))
    low = number - 64.0 * high
    named = iota((n_sub, chans), 0).astype(F32) == own
    digits = jnp.concatenate([jnp.where(named, high, 0.0), jnp.where(named, low, 0.0)], axis=0).astype(BF16)
    shifted = rank_col + (me * slots).astype(F32)
    place = one_hot(iota((chans, lanes), 1).astype(F32) == shifted)
    numbers = dot(digits, place)
    numbers = numbers[:n_sub] * 64.0 + numbers[n_sub:]
    for d in range(n_sub):
        idx_send[d] = numbers[d : d + 1]
    slot = own * float(slots) + rank
    select = one_hot(iota((n_sub * slots, chans), 0).astype(F32) == slot)
    packed = dot(select, meas[...])
    for d in range(n_sub):
        rows = packed[d * slots : (d + 1) * slots]
        pack_send[d] = jnp.concatenate([rows[:, :half], rows[:, half:]], axis=0).astype(BF16)

    pl.semaphore_wait(barrier, n_sub - 1 + n_freq - 1)

    def idx_copy(j):
        dest = lax.rem(me + j, n_sub)
        return pltpu.make_async_remote_copy(
            src_ref=idx_send.at[dest], dst_ref=idx_recv.at[me],
            send_sem=idx_ss.at[dest], recv_sem=idx_rs.at[me],
            device_id={"sub": dest}, device_id_type=MESH,
        )

    def pack_copy(j):
        dest = lax.rem(me + j, n_sub)
        return pltpu.make_async_remote_copy(
            src_ref=pack_send.at[dest], dst_ref=pack_recv.at[me],
            send_sem=pack_ss.at[dest], recv_sem=pack_rs.at[me],
            device_id={"sub": dest}, device_id_type=MESH,
        )

    far_first = sorted(range(1, n_sub), key=lambda j: abs(j - n_sub // 2))
    for j in far_first:
        idx_copy(j).start()
    for j in far_first:
        pack_copy(j).start()
    idx_recv[me] = idx_send[me]
    pack_recv[me] = pack_send[me]

    pad = ext_0.shape[1] - bs
    for buf in ext:
        buf[:, bs:, :] = jnp.zeros((nb + 2, pad, width), BF16)
    used = n_sub * slots
    if lanes > used:
        meas_all[used:, :] = jnp.zeros((lanes - used, width), F32)
    part[...] = jnp.zeros(part.shape, F32)

    @pl.when(me == 0)
    def _():
        for buf in ext:
            buf[0, :bs, :] = jnp.zeros((bs, width), BF16)

    @pl.when(me == n_sub - 1)
    def _():
        for buf in ext:
            buf[nb + 1, :bs, :] = jnp.zeros((bs, width), BF16)

    loads[0].wait()
    loads[1].wait()

    @pl.loop(0, nb // 4)
    def _(g):
        for i in range(4):
            b = g * 4 + i
            stiff_resp[b] = dot(stiff[b], resp[b])

    loads[2].wait()
    loads[3].wait()
    blank = jnp.zeros((2 * bs, LANES - bs), BF16)

    @pl.loop(0, nb)
    def _(b):
        tiles[b, :, :LANES] = jnp.concatenate([diag[b], blank], axis=1)
        for k in range(nnb):
            tiles[b, :, (k + 1) * LANES : (k + 2) * LANES] = jnp.concatenate([off[b, k], blank], axis=1)

    for j in range(1, n_sub):
        source = lax.rem(me + n_sub - j, n_sub)
        pltpu.make_async_remote_copy(
            src_ref=idx_send.at[source], dst_ref=idx_recv.at[source],
            send_sem=idx_ss.at[source], recv_sem=idx_rs.at[source],
            device_id={"sub": source}, device_id_type=MESH,
        ).wait_recv()
    numbers = idx_recv[0]
    for p in range(1, n_sub):
        numbers = numbers + idx_recv[p]
    numbers = jnp.broadcast_to(numbers - 1.0, (bs, lanes))

    @pl.loop(0, nb // 2)
    def _(g):
        for i in range(2):
            b = g * 2 + i
            here = iota((bs, lanes), 0).astype(F32) + (b * bs).astype(F32)
            hit = jnp.where(numbers == here, 1.0, 0.0)
            scat[b] = hit.astype(BF16)
            load[b] = jnp.sum(hit, axis=1, keepdims=True) * resp[b].astype(F32)

    loads[4].wait()
    for j in range(1, n_sub):
        source = lax.rem(me + n_sub - j, n_sub)
        pltpu.make_async_remote_copy(
            src_ref=pack_send.at[source], dst_ref=pack_recv.at[source],
            send_sem=pack_ss.at[source], recv_sem=pack_rs.at[source],
            device_id={"sub": source}, device_id_type=MESH,
        ).wait_recv()
    for p in range(n_sub):
        rows = pack_recv[p].astype(F32)
        meas_all[p * slots : (p + 1) * slots, :] = jnp.concatenate([rows[:slots], rows[slots:]], axis=1)
    rows_in = meas_all[...].astype(BF16)

    def halo(step, low):
        src = ext[step].at[1 if low else nb, pl.ds(0, bs)]
        dst = ext[step].at[nb + 1 if low else 0, pl.ds(0, bs)]
        target = lax.rem(me + (n_sub - 1 if low else 1), n_sub)
        way = 0 if low else 1
        return pltpu.make_async_remote_copy(
            src_ref=src, dst_ref=dst, send_sem=halo_ss.at[step, way], recv_sem=halo_rs.at[step, way],
            device_id={"sub": target}, device_id_type=MESH,
        )

    def halo_start(step):
        @pl.when(me > 0)
        def _():
            halo(step, True).start()

        @pl.when(me < n_sub - 1)
        def _():
            halo(step, False).start()

    def halo_wait(step):
        @pl.when(me > 0)
        def _():
            halo(step, False).wait_recv()

        @pl.when(me < n_sub - 1)
        def _():
            halo(step, True).wait_recv()

    def first(blocks):
        rhs = [load[b] - dot(scat[b], rows_in) for b in blocks]
        for b, value in zip(blocks, rhs):
            load[b] = value
        new = [combine(dot(prec[b], value.astype(BF16))) for b, value in zip(blocks, rhs)]
        for b, value in zip(blocks, new):
            lam[b] = value
            ext_0[b + 1, :bs, :] = value.astype(BF16)

    def sweep(step, blocks):
        updates = []
        for b in blocks:
            near = [ext[step][b + 1]] + [ext[step][cols[k, b]] for k in range(nnb)]
            prod = dot(tiles[b], jnp.concatenate(near, axis=0))
            updates.append((load[b] - combine(prod)).astype(BF16))
        new = [lam[b] + combine(dot(prec[b], value)) for b, value in zip(blocks, updates)]
        last = step == SWEEPS - 2
        for b, value in zip(blocks, new):
            if last:
                out[b] = value.astype(BF16)
                terms = jnp.sum(value * stiff_resp[b], axis=0, keepdims=True)
                part[pl.ds(b, 1), :] = terms[:, :half] + terms[:, half:]
            else:
                lam[b] = value
                ext[step + 1][b + 1, :bs, :] = value.astype(BF16)

    def inner(work):
        @pl.loop(0, (nb - 2) // group)
        def _(g):
            work([1 + g * group + i for i in range(group)])

    first([0, nb - 1])
    halo_start(0)
    inner(first)
    for step in range(SWEEPS - 1):
        halo_wait(step)
        sweep(step, [0, nb - 1])
        if step < SWEEPS - 2:
            halo_start(step + 1)
        inner(functools.partial(sweep, step))

    def part_copy(j):
        dest = lax.rem(fr + j, n_freq)
        return pltpu.make_async_remote_copy(
            src_ref=part, dst_ref=part_recv.at[fr],
            send_sem=part_ss.at[dest], recv_sem=part_rs.at[fr],
            device_id={"freq": dest}, device_id_type=MESH,
        )

    for j in range(1, n_freq):
        part_copy(j).start()
    part_recv[fr] = part[...]
    for j in range(1, n_sub):
        idx_copy(j).wait_send()
        pack_copy(j).wait_send()
    for step in range(SWEEPS - 1):
        @pl.when(me > 0)
        def _():
            halo(step, True).wait_send()

        @pl.when(me < n_sub - 1)
        def _():
            halo(step, False).wait_send()
    for j in range(1, n_freq):
        source = lax.rem(fr + n_freq - j, n_freq)
        pltpu.make_async_remote_copy(
            src_ref=part, dst_ref=part_recv.at[source],
            send_sem=part_ss.at[source], recv_sem=part_rs.at[source],
            device_id={"freq": source}, device_id_type=MESH,
        ).wait_recv()
    total = part_recv[0]
    for p in range(1, n_freq):
        total = total + part_recv[p]
    sums = jnp.sum(total, axis=1, keepdims=True) * (1.0 / math.sqrt(bs * width))
    mine = iota(total.shape, 0) == iota(total.shape, 1)
    line = jnp.sum(jnp.where(mine, sums, 0.0), axis=0, keepdims=True)
    grad[...] = line[:, :nb]
    for j in range(1, n_freq):
        part_copy(j).wait_send()


def shards(
    n_sub, n_freq,
    response, measured, sensor_owner, sensor_row, adj_diag, adj_off, block_cols, precond, stiff_deriv,
):
    _, nb, bs, width = response.shape
    nnb = adj_off.shape[2]
    chans = measured.shape[1]
    cap = min(CAPS.get(n_sub, chans), chans)
    slots = round_up(cap, 8)
    lanes = round_up(n_sub * slots, LANES)
    halves = SWEEPS - 1
    group = next(g for g in (5, 4, 3, 2, 1) if (nb - 2) % g == 0)
    dma = pltpu.SemaphoreType.DMA
    vmem = pl.BlockSpec(memory_space=pltpu.VMEM)
    hbm = pl.BlockSpec(memory_space=pl.ANY)
    adjoint, gradient = pl.pallas_call(
        functools.partial(kernel, n_sub, n_freq, slots, group),
        out_shape=(
            jax.ShapeDtypeStruct((nb, bs, width), BF16),
            jax.ShapeDtypeStruct((1, nb), F32),
        ),
        in_specs=[hbm, vmem, vmem, vmem, hbm, hbm, pl.BlockSpec(memory_space=pltpu.SMEM), hbm, hbm],
        out_specs=(vmem, vmem),
        scratch_shapes=[
            pltpu.VMEM((nb, bs, width), BF16),
            pltpu.VMEM((nb, 2 * bs, bs), BF16),
            pltpu.VMEM((nb, nnb, 2 * bs, bs), BF16),
            pltpu.VMEM((nb, 2 * bs, bs), BF16),
            pltpu.VMEM((nb, bs, bs), BF16),
            pltpu.VMEM((nb, 2 * bs, (nnb + 1) * LANES), BF16),
            pltpu.VMEM((nb + 2, LANES, width), BF16),
            pltpu.VMEM((nb + 2, LANES, width), BF16),
            pltpu.VMEM((nb, bs, width), F32),
            pltpu.VMEM((nb, bs, width), F32),
            pltpu.VMEM((nb, bs, width), F32),
            pltpu.VMEM((nb, bs, lanes), BF16),
            pltpu.VMEM((n_sub, 1, lanes), F32),
            pltpu.VMEM((n_sub, 1, lanes), F32),
            pltpu.VMEM((n_sub, 2 * slots, width // 2), BF16),
            pltpu.VMEM((n_sub, 2 * slots, width // 2), BF16),
            pltpu.VMEM((lanes, width), F32),
            pltpu.VMEM((round_up(nb, 8), width // 2), F32),
            pltpu.VMEM((n_freq, round_up(nb, 8), width // 2), F32),
            dma((5,)),
            dma((n_sub,)), dma((n_sub,)),
            dma((n_sub,)), dma((n_sub,)),
            dma((halves, 2)), dma((halves, 2)),
            dma((n_freq,)), dma((n_freq,)),
        ],
        compiler_params=pltpu.CompilerParams(
            collective_id=0, has_side_effects=True, vmem_limit_bytes=48 * 1024 * 1024
        ),
        name="adjoint_sweeps",
    )(
        response.reshape(nb, bs, width),
        measured.reshape(chans, width),
        sensor_owner.reshape(1, chans),
        sensor_row.reshape(1, chans),
        adj_diag.reshape(nb, 2 * bs, bs),
        adj_off.reshape(nb, nnb, 2 * bs, bs),
        block_cols.T,
        precond.reshape(nb, 2 * bs, bs),
        stiff_deriv,
    )
    return adjoint[None], gradient.reshape(nb)


def solution(mesh):
    in_specs = (
        P("freq", "sub", None, None),
        P("freq", "sub", None),
        P("sub"),
        P("sub"),
        P("freq", "sub", None, None, None),
        P("freq", "sub", None, None, None, None),
        P("sub", None),
        P("freq", "sub", None, None, None),
        P("sub", None, None),
    )
    out_specs = (P("freq", "sub", None, None), P("sub"))
    body = functools.partial(shards, mesh.shape["sub"], mesh.shape["freq"])
    return jax.shard_map(body, mesh=mesh, in_specs=in_specs, out_specs=out_specs, check_vma=False)
```

time: 119 us -> 36.4 us (0.31)
  blocking collectives: 50.7 us -> 0 us
  Pallas kernels: 0 us -> 25.2 us
  other arithmetic: 19.5 us -> 0 us
  matrix products: 15.6 us -> 0 us
  starting transfers between devices: 9.2 us -> 0 us
  local copies, waits for them, and re-layouts: 18.7 us -> 10.1 us
  waiting for transfers between devices: 3.28 us -> 0 us
    all_gather x1 -> x0, blocking collectives: 31.4 us -> none  [shards(): lax.all_gather(local_measurements, 'sub', axis=0, tiled=True)]
    pallas_call x0 -> x1, Pallas kernels: none -> 25.2 us  [shards(): pl.pallas_call(functools.partial(kernel, n_sub, n_freq, slots, group), ou...]
    dot_general x15 -> x0, matrix products: 15.6 us -> none  [the longest x2 6.15 us: coupled_apply(): jnp.einsum('bkij,bkjn->bin', tile_set[:, :, 1], gathered, preferred_eleme...]
    unnamed x1 -> x0, blocking collectives: 13.2 us -> none
    scatter-add x1 -> x0, other arithmetic: 10.9 us -> none  [shards(): load_flat = empty_load.at[safe_index].add(misfit)]
    ppermute x4 -> x0, starting transfers between devices: 9.2 us -> none  [the longest x2 6.45 us: with_halo(): lax.ppermute(lax.slice_in_dim(block, block.shape[dim] - width, None, axis...]
    psum x1 -> x0, blocking collectives: 6.16 us -> none  [shards(): gradient = lax.psum(partial_grad, 'freq')]
    gather x2 -> x0, local copies, waits for them, and re-layouts: 4.75 us -> none  [shards(): gathered = extended[block_cols]]
  transfers between devices with their start and end apart: 4 -> 0, of which waited for: 1 -> 0; matrix products, arithmetic and copies ran while one was open for 6% -> 0% of each run, Pallas kernels for 0% -> 0%
where the time goes in v1:
time: 36.4 us; the launch traced here: 35.9 us
  Pallas kernels  25.2 us (69%)
  local copies, waits for them, and re-layouts  10.1 us (28%)
  between operations  0.66 us (2%)
    pallas_call x1, Pallas kernels, shards(): pl.pallas_call(functools.partial(kernel, n_sub, n_freq, slots, group), ou...  25.2 us
    unnamed x20, local copies, waits for them, and re-layouts  10.1 us

profile of v1, /device:TPU:0, one launch (start us, length us, event | category | flops | bytes accessed | tf_op | source)
XLA Modules:
  0.0 35.9 jit_solution(9090828965075425927)
XLA Ops:
  0.6 0.0 copy-start
  0.6 1.8 %copy-done = bf16[1,12,5,2,96,96]{5,4,3,2,1,0:T(8,128)(2,1)S(1)} copy-done((bf16[1,12,5,2,96,96]{5,4,3,2,1,0:T(8,128)(2,1)S(1)}, bf16[1,12,5,2,96,96]{5,4,3,2,1,0:T(8,128)(2,1)}, u32[]{:S(2)}) %copy-start) | copy-done | bytes 2211864
  2.5 0.0 copy-start.1
  2.5 1.1 %copy-done.1 = bf16[1,12,96,256]{3,2,1,0:T(8,128)(2,1)S(1)} copy-done((bf16[1,12,96,256]{3,2,1,0:T(8,128)(2,1)S(1)}, bf16[1,12,96,256]{3,2,1,0:T(8,128)(2,1)}, u32[]{:S(2)}) %copy-start.1) | copy-done | bytes 589848
  3.5 0.0 copy-start.2
  3.5 1.1 %copy-done.2 = bf16[1,12,2,96,96]{4,3,2,1,0:T(8,128)(2,1)S(1)} copy-done((bf16[1,12,2,96,96]{4,3,2,1,0:T(8,128)(2,1)S(1)}, bf16[1,12,2,96,96]{4,3,2,1,0:T(8,128)(2,1)}, u32[]{:S(2)}) %copy-start.2) | copy-done | bytes 442392
  4.6 0.0 copy-start.3
  4.6 1.1 %copy-done.3 = bf16[1,12,2,96,96]{4,3,2,1,0:T(8,128)(2,1)S(1)} copy-done((bf16[1,12,2,96,96]{4,3,2,1,0:T(8,128)(2,1)S(1)}, bf16[1,12,2,96,96]{4,3,2,1,0:T(8,128)(2,1)}, u32[]{:S(2)}) %copy-start.3) | copy-done | bytes 442392
  5.7 0.0 copy-start.4
  5.7 1.0 %copy-done.4 = bf16[12,96,96]{2,1,0:T(8,128)(2,1)S(1)} copy-done((bf16[12,96,96]{2,1,0:T(8,128)(2,1)S(1)}, bf16[12,96,96]{2,1,0:T(8,128)(2,1)}, u32[]{:S(2)}) %copy-start.4) | copy-done | bytes 221208
  6.6 0.0 copy-start.5
  6.6 0.8 %copy-done.5 = bf16[1,96,256]{2,1,0:T(8,128)(2,1)S(1)} copy-done((bf16[1,96,256]{2,1,0:T(8,128)(2,1)S(1)}, bf16[1,96,256]{2,1,0:T(8,128)(2,1)}, u32[]{:S(2)}) %copy-start.5) | copy-done | bytes 49176
  7.4 0.0 copy-start.6
  7.4 0.7 %copy-done.6 = s32[12,5]{0,1:T(8,128)S(1)} copy-done((s32[12,5]{0,1:T(8,128)S(1)}, s32[12,5]{0,1:T(8,128)}, u32[]{:S(2)}) %copy-start.6) | copy-done | bytes 264
  8.1 0.0 copy-start.7
  8.1 0.7 %copy-done.7 = s32[96]{0:T(128)S(1)} copy-done((s32[96]{0:T(128)S(1)}, s32[96]{0:T(128)}, u32[]{:S(2)}) %copy-start.7) | copy-done | bytes 408
  8.8 0.0 copy-start.8
  8.8 0.7 %copy-done.8 = s32[96]{0:T(128)S(1)} copy-done((s32[96]{0:T(128)S(1)}, s32[96]{0:T(128)}, u32[]{:S(2)}) %copy-start.8) | copy-done | bytes 408
  9.4 25.2 %adjoint_sweeps.1 = (bf16[12,96,256]{2,1,0:T(8,128)(2,1)S(1)}, f32[1,12]{1,0:T(1,128)S(1)}) custom-call(bf16[12,96,256]{2,1,0:T(8,128)(2,1)S(1)} %bitcast.11, bf16[96,256]{1,0:T(8,128)(2,1)S(1)} %bitcast.15, s32[1,96]{1,0:T(1,128)S(1)} %bitcast.17, s32[1,96]{1,0:T(1,128)S(1)} %bitcast.18, bf16[12,192,96]{2,1,0:T(8,128)(2,1)S(1)} %bitcast.12, ...), custom_call_target="tpu_custom_call" | custom-call | tf_op jit(solution)/shard_map/adjoint_sweeps/pallas_call | solution.py:320
  34.6 0.8 %copy.13 = bf16[1,12,96,256]{3,2,1,0:T(8,128)(2,1)} copy(bf16[1,12,96,256]{3,2,1,0:T(8,128)(2,1)S(1)} %bitcast.14) | data formatting | bytes 1179648
  35.4 0.5 %copy.14 = f32[12]{0:T(128)} copy(f32[12]{0:T(128)S(1)} %bitcast.19) | data formatting | bytes 96
Async XLA Ops:
  0.6 1.8 %copy-start = (bf16[1,12,5,2,96,96]{5,4,3,2,1,0:T(8,128)(2,1)S(1)}, bf16[1,12,5,2,96,96]{5,4,3,2,1,0:T(8,128)(2,1)}, u32[]{:S(2)}) copy-start(bf16[1,12,5,2,96,96]{5,4,3,2,1,0:T(8,128)(2,1)} %param.14) | copy-start | bytes 6635524
  2.5 1.1 %copy-start.1 = (bf16[1,12,96,256]{3,2,1,0:T(8,128)(2,1)S(1)}, bf16[1,12,96,256]{3,2,1,0:T(8,128)(2,1)}, u32[]{:S(2)}) copy-start(bf16[1,12,96,256]{3,2,1,0:T(8,128)(2,1)} %param.9) | copy-start | bytes 1769476
  3.5 1.1 %copy-start.2 = (bf16[1,12,2,96,96]{4,3,2,1,0:T(8,128)(2,1)S(1)}, bf16[1,12,2,96,96]{4,3,2,1,0:T(8,128)(2,1)}, u32[]{:S(2)}) copy-start(bf16[1,12,2,96,96]{4,3,2,1,0:T(8,128)(2,1)} %param.13) | copy-start | bytes 1327108
  4.6 1.1 %copy-start.3 = (bf16[1,12,2,96,96]{4,3,2,1,0:T(8,128)(2,1)S(1)}, bf16[1,12,2,96,96]{4,3,2,1,0:T(8,128)(2,1)}, u32[]{:S(2)}) copy-start(bf16[1,12,2,96,96]{4,3,2,1,0:T(8,128)(2,1)} %param.16) | copy-start | bytes 1327108
  5.7 1.0 %copy-start.4 = (bf16[12,96,96]{2,1,0:T(8,128)(2,1)S(1)}, bf16[12,96,96]{2,1,0:T(8,128)(2,1)}, u32[]{:S(2)}) copy-start(bf16[12,96,96]{2,1,0:T(8,128)(2,1)} %stiff_hbm.1) | copy-start | bytes 663556
  6.6 0.8 %copy-start.5 = (bf16[1,96,256]{2,1,0:T(8,128)(2,1)S(1)}, bf16[1,96,256]{2,1,0:T(8,128)(2,1)}, u32[]{:S(2)}) copy-start(bf16[1,96,256]{2,1,0:T(8,128)(2,1)} %param.10) | copy-start | bytes 147460
  7.4 0.7 %copy-start.6 = (s32[12,5]{0,1:T(8,128)S(1)}, s32[12,5]{0,1:T(8,128)}, u32[]{:S(2)}) copy-start(s32[12,5]{0,1:T(8,128)} %param.15) | copy-start | bytes 724
  8.1 0.7 %copy-start.7 = (s32[96]{0:T(128)S(1)}, s32[96]{0:T(128)}, u32[]{:S(2)}) copy-start(s32[96]{0:T(128)} %param.11) | copy-start | bytes 1156
  8.8 0.7 %copy-start.8 = (s32[96]{0:T(128)S(1)}, s32[96]{0:T(128)}, u32[]{:S(2)}) copy-start(s32[96]{0:T(128)} %param.12) | copy-start | bytes 1156

commit v2 on v1

--- a/solution.py
+++ b/solution.py
@@ -41,11 +41,11 @@
 
 def kernel(
     n_sub, n_freq, slots, group,
-    resp_hbm, meas, owner, row, diag_hbm, off_hbm, cols, prec_hbm, stiff_hbm,
-    out, grad,
-    resp, diag, off, prec, stiff, tiles, ext_0, ext_1, load, lam, stiff_resp, scat,
+    resp_hbm, meas_hbm, owner_hbm, row_hbm, diag_hbm, off_hbm, cols_hbm, prec_hbm, stiff_hbm,
+    out_hbm, grad,
+    out, meas, owner, row, cols, resp, diag, off, prec, stiff, tiles, ext_0, ext_1, load, lam, stiff_resp, scat,
     idx_send, idx_recv, pack_send, pack_recv, meas_all, part, part_recv,
-    in_sem, idx_ss, idx_rs, pack_ss, pack_rs, halo_ss, halo_rs, part_ss, part_rs,
+    in_sem, out_sem, idx_ss, idx_rs, pack_ss, pack_rs, halo_ss, halo_rs, part_ss, part_rs,
 ):
     nb, bs, width = resp.shape
     nnb = off.shape[1]
@@ -59,7 +59,10 @@
     loads = [
         pltpu.make_async_copy(src, dst, in_sem.at[i])
         for i, (src, dst) in enumerate(
-            [(resp_hbm, resp), (stiff_hbm, stiff), (diag_hbm, diag), (off_hbm, off), (prec_hbm, prec)]
+            [
+                (owner_hbm, owner), (row_hbm, row), (meas_hbm, meas), (resp_hbm, resp), (stiff_hbm, stiff),
+                (diag_hbm, diag), (off_hbm, off), (prec_hbm, prec), (cols_hbm, cols),
+            ]
         )
     ]
     for copy in loads:
@@ -71,6 +74,8 @@
     for j in range(1, n_freq):
         pl.semaphore_signal(barrier, inc=1, device_id={"freq": lax.rem(fr + j, n_freq)}, device_id_type=MESH)
 
+    loads[0].wait()
+    loads[1].wait()
     own = owner[...].astype(F32)
     ri, ci = iota((chans, chans), 0), iota((chans, chans), 1)
     own_b = jnp.broadcast_to(own, (chans, chans))
@@ -91,6 +96,7 @@
         idx_send[d] = numbers[d : d + 1]
     slot = own * float(slots) + rank
     select = one_hot(iota((n_sub * slots, chans), 0).astype(F32) == slot)
+    loads[2].wait()
     packed = dot(select, meas[...])
     for d in range(n_sub):
         rows = packed[d * slots : (d + 1) * slots]
@@ -140,8 +146,8 @@
         for buf in ext:
             buf[nb + 1, :bs, :] = jnp.zeros((bs, width), BF16)
 
-    loads[0].wait()
-    loads[1].wait()
+    loads[3].wait()
+    loads[4].wait()
 
     @pl.loop(0, nb // 4)
     def _(g):
@@ -149,15 +155,16 @@
             b = g * 4 + i
             stiff_resp[b] = dot(stiff[b], resp[b])
 
-    loads[2].wait()
-    loads[3].wait()
-    blank = jnp.zeros((2 * bs, LANES - bs), BF16)
+    loads[5].wait()
+    loads[6].wait()
+    for k in range(nnb + 1):
+        tiles[:, :, k * LANES + bs : (k + 1) * LANES] = jnp.zeros((nb, 2 * bs, LANES - bs), BF16)
 
     @pl.loop(0, nb)
     def _(b):
-        tiles[b, :, :LANES] = jnp.concatenate([diag[b], blank], axis=1)
+        tiles[b, :, :bs] = diag[b]
         for k in range(nnb):
-            tiles[b, :, (k + 1) * LANES : (k + 2) * LANES] = jnp.concatenate([off[b, k], blank], axis=1)
+            tiles[b, :, (k + 1) * LANES : (k + 1) * LANES + bs] = off[b, k]
 
     for j in range(1, n_sub):
         source = lax.rem(me + n_sub - j, n_sub)
@@ -180,7 +187,8 @@
             scat[b] = hit.astype(BF16)
             load[b] = jnp.sum(hit, axis=1, keepdims=True) * resp[b].astype(F32)
 
-    loads[4].wait()
+    loads[7].wait()
+    loads[8].wait()
     for j in range(1, n_sub):
         source = lax.rem(me + n_sub - j, n_sub)
         pltpu.make_async_remote_copy(
@@ -230,6 +238,9 @@
             lam[b] = value
             ext_0[b + 1, :bs, :] = value.astype(BF16)
 
+    def out_copy(b):
+        return pltpu.make_async_copy(out.at[b], out_hbm.at[b], out_sem.at[b])
+
     def sweep(step, blocks):
         updates = []
         for b in blocks:
@@ -241,6 +252,7 @@
         for b, value in zip(blocks, new):
             if last:
                 out[b] = value.astype(BF16)
+                out_copy(b).start()
                 terms = jnp.sum(value * stiff_resp[b], axis=0, keepdims=True)
                 part[pl.ds(b, 1), :] = terms[:, :half] + terms[:, half:]
             else:
@@ -257,10 +269,14 @@
     inner(first)
     for step in range(SWEEPS - 1):
         halo_wait(step)
-        sweep(step, [0, nb - 1])
         if step < SWEEPS - 2:
+            sweep(step, [0, nb - 1])
             halo_start(step + 1)
-        inner(functools.partial(sweep, step))
+            inner(functools.partial(sweep, step))
+        else:
+            @pl.loop(0, nb // 4)
+            def _(g):
+                sweep(step, [g * 4 + i for i in range(4)])
 
     def part_copy(j):
         dest = lax.rem(fr + j, n_freq)
@@ -298,6 +314,8 @@
     mine = iota(total.shape, 0) == iota(total.shape, 1)
     line = jnp.sum(jnp.where(mine, sums, 0.0), axis=0, keepdims=True)
     grad[...] = line[:, :nb]
+    for b in range(nb):
+        out_copy(b).wait()
     for j in range(1, n_freq):
         part_copy(j).wait_send()
 
@@ -316,16 +334,21 @@
     group = next(g for g in (5, 4, 3, 2, 1) if (nb - 2) % g == 0)
     dma = pltpu.SemaphoreType.DMA
     vmem = pl.BlockSpec(memory_space=pltpu.VMEM)
-    hbm = pl.BlockSpec(memory_space=pl.ANY)
+    hbm = pl.BlockSpec(memory_space=pltpu.HBM)
     adjoint, gradient = pl.pallas_call(
         functools.partial(kernel, n_sub, n_freq, slots, group),
         out_shape=(
             jax.ShapeDtypeStruct((nb, bs, width), BF16),
             jax.ShapeDtypeStruct((1, nb), F32),
         ),
-        in_specs=[hbm, vmem, vmem, vmem, hbm, hbm, pl.BlockSpec(memory_space=pltpu.SMEM), hbm, hbm],
-        out_specs=(vmem, vmem),
+        in_specs=[hbm] * 9,
+        out_specs=(hbm, vmem),
         scratch_shapes=[
+            pltpu.VMEM((nb, bs, width), BF16),
+            pltpu.VMEM((chans, width), BF16),
+            pltpu.VMEM((1, chans), jnp.int32),
+            pltpu.VMEM((1, chans), jnp.int32),
+            pltpu.SMEM((nnb, nb), jnp.int32),
             pltpu.VMEM((nb, bs, width), BF16),
             pltpu.VMEM((nb, 2 * bs, bs), BF16),
             pltpu.VMEM((nb, nnb, 2 * bs, bs), BF16),
@@ -345,14 +368,14 @@
             pltpu.VMEM((lanes, width), F32),
             pltpu.VMEM((round_up(nb, 8), width // 2), F32),
             pltpu.VMEM((n_freq, round_up(nb, 8), width // 2), F32),
-            dma((5,)),
+            dma((9,)), dma((nb,)),
             dma((n_sub,)), dma((n_sub,)),
             dma((n_sub,)), dma((n_sub,)),
             dma((halves, 2)), dma((halves, 2)),
             dma((n_freq,)), dma((n_freq,)),
         ],
         compiler_params=pltpu.CompilerParams(
-            collective_id=0, has_side_effects=True, vmem_limit_bytes=48 * 1024 * 1024
+            collective_id=0, has_side_effects=True, vmem_limit_bytes=60 * 1024 * 1024
         ),
         name="adjoint_sweeps",
     )(

time: 36.4 us -> 28.7 us (0.79)
  local copies, waits for them, and re-layouts: 10.1 us -> 3.09 us
  Pallas kernels: 25.2 us -> 24.8 us
    unnamed x20 -> x2, local copies, waits for them, and re-layouts: 10.1 us -> 3.09 us
    pallas_call x1, Pallas kernels: 25.2 us -> 24.8 us  [shards(): pl.pallas_call(functools.partial(kernel, n_sub, n_freq, slots, group), ou...]
where the time goes in v2:
time: 28.7 us; the launch traced here: 28.5 us
  Pallas kernels  24.8 us (86%)
  local copies, waits for them, and re-layouts  3.09 us (11%)
  between operations  0.64 us (2%)
    pallas_call x1, Pallas kernels, shards(): pl.pallas_call(functools.partial(kernel, n_sub, n_freq, slots, group), ou...  24.8 us
    unnamed x2, local copies, waits for them, and re-layouts  3.09 us

profile of v2, /device:TPU:0, one launch (start us, length us, event | category | flops | bytes accessed | tf_op | source)
XLA Modules:
  0.0 28.5 jit_solution(16173371529442491272)
XLA Ops:
  0.6 24.8 %adjoint_sweeps.1 = (bf16[12,96,256]{2,1,0:T(8,128)(2,1)}, f32[1,12]{1,0:T(1,128)}) custom-call(bf16[12,96,256]{2,1,0:T(8,128)(2,1)} %bitcast.11, bf16[96,256]{1,0:T(8,128)(2,1)} %bitcast.15, s32[1,96]{1,0:T(1,128)} %bitcast.17, s32[1,96]{1,0:T(1,128)} %bitcast.18, bf16[12,192,96]{2,1,0:T(8,128)(2,1)} %bitcast.12, bf16[12,5,192,96]{3,2,1,0:T(8,128)(2,1)} %bitcast.10, ...), custom_call_target="tpu_custom_call" | custom-call | tf_op jit(solution)/shard_map/adjoint_sweeps/pallas_call | solution.py:338
  25.4 1.9 %copy.13 = bf16[1,12,96,256]{3,2,1,0:T(8,128)(2,1)} copy(bf16[1,12,96,256]{3,2,1,0:T(8,128)(2,1)} %bitcast.14) | data formatting | bytes 1179648
  27.3 1.2 %copy.14 = f32[12]{0:T(128)} copy(f32[12]{0:T(128)} %bitcast.19) | data formatting | bytes 96

commit v3 on v2

--- a/solution.py
+++ b/solution.py
@@ -42,15 +42,15 @@
 def kernel(
     n_sub, n_freq, slots, group,
     resp_hbm, meas_hbm, owner_hbm, row_hbm, diag_hbm, off_hbm, cols_hbm, prec_hbm, stiff_hbm,
-    out_hbm, grad,
-    out, meas, owner, row, cols, resp, diag, off, prec, stiff, tiles, ext_0, ext_1, load, lam, stiff_resp, scat,
+    out, grad,
+    meas, owner, row, cols, resp, diag, off, prec, stiff, tiles, edge_tiles, ext_0, ext_1, hal_0, hal_1, load, rest, lam, stiff_resp, scat,
     idx_send, idx_recv, pack_send, pack_recv, meas_all, part, part_recv,
-    in_sem, out_sem, idx_ss, idx_rs, pack_ss, pack_rs, halo_ss, halo_rs, part_ss, part_rs,
+    in_sem, idx_ss, idx_rs, pack_ss, pack_rs, halo_ss, halo_rs, part_ss, part_rs,
 ):
     nb, bs, width = resp.shape
     nnb = off.shape[1]
     half = width // 2
-    ext = (ext_0, ext_1)
+    ext, hal = (ext_0, ext_1), (hal_0, hal_1)
     chans = meas.shape[0]
     lanes = scat.shape[2]
     me = lax.axis_index("sub")
@@ -73,6 +73,32 @@
         pl.semaphore_signal(barrier, inc=1, device_id={"sub": lax.rem(me + j, n_sub)}, device_id_type=MESH)
     for j in range(1, n_freq):
         pl.semaphore_signal(barrier, inc=1, device_id={"freq": lax.rem(fr + j, n_freq)}, device_id_type=MESH)
+
+    pad = LANES - bs
+    for buf in ext:
+        buf[:, bs:, :] = jnp.zeros((nb + 2, pad, width), BF16)
+        for end in (0, nb + 1):
+            buf[end, :bs, :] = jnp.zeros((bs, width), BF16)
+    for buf in hal:
+        buf[:, bs:, :] = jnp.zeros((2, pad, width), BF16)
+    for k in range(nnb + 1):
+        tiles[:, :, k * LANES + bs : (k + 1) * LANES] = jnp.zeros((nb, 2 * bs, pad), BF16)
+    for k in range(2):
+        edge_tiles[:, :, k * LANES + bs : (k + 1) * LANES] = jnp.zeros((nb, 2 * bs, pad), BF16)
+    used = n_sub * slots
+    if lanes > used:
+        meas_all[used:, :] = jnp.zeros((lanes - used, width), F32)
+    part[...] = jnp.zeros(part.shape, F32)
+
+    @pl.when(me == 0)
+    def _():
+        for buf in hal:
+            buf[0, :bs, :] = jnp.zeros((bs, width), BF16)
+
+    @pl.when(me == n_sub - 1)
+    def _():
+        for buf in hal:
+            buf[1, :bs, :] = jnp.zeros((bs, width), BF16)
 
     loads[0].wait()
     loads[1].wait()
@@ -128,24 +154,6 @@
     idx_recv[me] = idx_send[me]
     pack_recv[me] = pack_send[me]
 
-    pad = ext_0.shape[1] - bs
-    for buf in ext:
-        buf[:, bs:, :] = jnp.zeros((nb + 2, pad, width), BF16)
-    used = n_sub * slots
-    if lanes > used:
-        meas_all[used:, :] = jnp.zeros((lanes - used, width), F32)
-    part[...] = jnp.zeros(part.shape, F32)
-
-    @pl.when(me == 0)
-    def _():
-        for buf in ext:
-            buf[0, :bs, :] = jnp.zeros((bs, width), BF16)
-
-    @pl.when(me == n_sub - 1)
-    def _():
-        for buf in ext:
-            buf[nb + 1, :bs, :] = jnp.zeros((bs, width), BF16)
-
     loads[3].wait()
     loads[4].wait()
 
@@ -157,14 +165,18 @@
 
     loads[5].wait()
     loads[6].wait()
-    for k in range(nnb + 1):
-        tiles[:, :, k * LANES + bs : (k + 1) * LANES] = jnp.zeros((nb, 2 * bs, LANES - bs), BF16)
+    loads[8].wait()
 
     @pl.loop(0, nb)
     def _(b):
         tiles[b, :, :bs] = diag[b]
         for k in range(nnb):
             tiles[b, :, (k + 1) * LANES : (k + 1) * LANES + bs] = off[b, k]
+        for side, column in enumerate((0, nb + 1)):
+            total = jnp.zeros((2 * bs, bs), F32)
+            for k in range(nnb):
+                total = total + jnp.where(cols[k, b] == column, 1.0, 0.0) * off[b, k].astype(F32)
+            edge_tiles[b, :, side * LANES : side * LANES + bs] = total.astype(BF16)
 
     for j in range(1, n_sub):
         source = lax.rem(me + n_sub - j, n_sub)
@@ -188,7 +200,6 @@
             load[b] = jnp.sum(hit, axis=1, keepdims=True) * resp[b].astype(F32)
 
     loads[7].wait()
-    loads[8].wait()
     for j in range(1, n_sub):
         source = lax.rem(me + n_sub - j, n_sub)
         pltpu.make_async_remote_copy(
@@ -203,7 +214,7 @@
 
     def halo(step, low):
         src = ext[step].at[1 if low else nb, pl.ds(0, bs)]
-        dst = ext[step].at[nb + 1 if low else 0, pl.ds(0, bs)]
+        dst = hal[step].at[1 if low else 0, pl.ds(0, bs)]
         target = lax.rem(me + (n_sub - 1 if low else 1), n_sub)
         way = 0 if low else 1
         return pltpu.make_async_remote_copy(
@@ -238,21 +249,22 @@
             lam[b] = value
             ext_0[b + 1, :bs, :] = value.astype(BF16)
 
-    def out_copy(b):
-        return pltpu.make_async_copy(out.at[b], out_hbm.at[b], out_sem.at[b])
-
-    def sweep(step, blocks):
-        updates = []
+    def interior(step, blocks):
+        values = []
         for b in blocks:
             near = [ext[step][b + 1]] + [ext[step][cols[k, b]] for k in range(nnb)]
-            prod = dot(tiles[b], jnp.concatenate(near, axis=0))
-            updates.append((load[b] - combine(prod)).astype(BF16))
+            values.append(load[b] - combine(dot(tiles[b], jnp.concatenate(near, axis=0))))
+        for b, value in zip(blocks, values):
+            rest[b] = value
+
+    def finish(step, blocks):
+        beside = hal[step][...].reshape(2 * LANES, width)
+        updates = [(rest[b] - combine(dot(edge_tiles[b], beside))).astype(BF16) for b in blocks]
         new = [lam[b] + combine(dot(prec[b], value)) for b, value in zip(blocks, updates)]
         last = step == SWEEPS - 2
         for b, value in zip(blocks, new):
             if last:
                 out[b] = value.astype(BF16)
-                out_copy(b).start()
                 terms = jnp.sum(value * stiff_resp[b], axis=0, keepdims=True)
                 part[pl.ds(b, 1), :] = terms[:, :half] + terms[:, half:]
             else:
@@ -264,19 +276,23 @@
         def _(g):
             work([1 + g * group + i for i in range(group)])
 
+    def every(work):
+        @pl.loop(0, nb // 4)
+        def _(g):
+            work([g * 4 + i for i in range(4)])
+
     first([0, nb - 1])
     halo_start(0)
     inner(first)
     for step in range(SWEEPS - 1):
+        every(functools.partial(interior, step))
         halo_wait(step)
         if step < SWEEPS - 2:
-            sweep(step, [0, nb - 1])
+            finish(step, [0, nb - 1])
             halo_start(step + 1)
-            inner(functools.partial(sweep, step))
+            inner(functools.partial(finish, step))
         else:
-            @pl.loop(0, nb // 4)
-            def _(g):
-                sweep(step, [g * 4 + i for i in range(4)])
+            every(functools.partial(finish, step))
 
     def part_copy(j):
         dest = lax.rem(fr + j, n_freq)
@@ -314,8 +330,6 @@
     mine = iota(total.shape, 0) == iota(total.shape, 1)
     line = jnp.sum(jnp.where(mine, sums, 0.0), axis=0, keepdims=True)
     grad[...] = line[:, :nb]
-    for b in range(nb):
-        out_copy(b).wait()
     for j in range(1, n_freq):
         part_copy(j).wait_send()
 
@@ -342,9 +356,8 @@
             jax.ShapeDtypeStruct((1, nb), F32),
         ),
         in_specs=[hbm] * 9,
-        out_specs=(hbm, vmem),
+        out_specs=(vmem, vmem),
         scratch_shapes=[
-            pltpu.VMEM((nb, bs, width), BF16),
             pltpu.VMEM((chans, width), BF16),
             pltpu.VMEM((1, chans), jnp.int32),
             pltpu.VMEM((1, chans), jnp.int32),
@@ -355,8 +368,12 @@
             pltpu.VMEM((nb, 2 * bs, bs), BF16),
             pltpu.VMEM((nb, bs, bs), BF16),
             pltpu.VMEM((nb, 2 * bs, (nnb + 1) * LANES), BF16),
+            pltpu.VMEM((nb, 2 * bs, 2 * LANES), BF16),
             pltpu.VMEM((nb + 2, LANES, width), BF16),
             pltpu.VMEM((nb + 2, LANES, width), BF16),
+            pltpu.VMEM((2, LANES, width), BF16),
+            pltpu.VMEM((2, LANES, width), BF16),
+            pltpu.VMEM((nb, bs, width), F32),
             pltpu.VMEM((nb, bs, width), F32),
             pltpu.VMEM((nb, bs, width), F32),
             pltpu.VMEM((nb, bs, width), F32),
@@ -368,17 +385,17 @@
             pltpu.VMEM((lanes, width), F32),
             pltpu.VMEM((round_up(nb, 8), width // 2), F32),
             pltpu.VMEM((n_freq, round_up(nb, 8), width // 2), F32),
-            dma((9,)), dma((nb,)),
+            dma((9,)),
             dma((n_sub,)), dma((n_sub,)),
             dma((n_sub,)), dma((n_sub,)),
             dma((halves, 2)), dma((halves, 2)),
             dma((n_freq,)), dma((n_freq,)),
         ],
         compiler_params=pltpu.CompilerParams(
-            collective_id=0, has_side_effects=True, vmem_limit_bytes=60 * 1024 * 1024
+            collective_id=0, has_side_effects=True, vmem_limit_bytes=48 * 1024 * 1024
         ),
         name="adjoint_sweeps",
-    )(
+    )(*(pltpu.with_memory_space_constraint(x, pltpu.HBM) for x in (
         response.reshape(nb, bs, width),
         measured.reshape(chans, width),
         sensor_owner.reshape(1, chans),
@@ -388,7 +405,7 @@
         block_cols.T,
         precond.reshape(nb, 2 * bs, bs),
         stiff_deriv,
-    )
+    )))
     return adjoint[None], gradient.reshape(nb)
 
 

time: 28.7 us -> 25.4 us (0.89)
  local copies, waits for them, and re-layouts: 3.09 us -> 1.33 us
  Pallas kernels: 24.8 us -> 23.3 us
    unnamed x2, local copies, waits for them, and re-layouts: 3.09 us -> 1.33 us
    pallas_call x1, Pallas kernels: 24.8 us -> 23.3 us  [shards(): pl.pallas_call(functools.partial(kernel, n_sub, n_freq, slots, group), ou...]
where the time goes in v3:
time: 25.4 us; the launch traced here: 25.3 us
  Pallas kernels  23.3 us (92%)
  local copies, waits for them, and re-layouts  1.33 us (5%)
  between operations  0.64 us (3%)
    pallas_call x1, Pallas kernels, shards(): pl.pallas_call(functools.partial(kernel, n_sub, n_freq, slots, group), ou...  23.3 us
    unnamed x2, local copies, waits for them, and re-layouts  1.33 us

profile of v3, /device:TPU:0, one launch (start us, length us, event | category | flops | bytes accessed | tf_op | source)
XLA Modules:
  0.0 25.3 jit_solution(17124907328945845583)
XLA Ops:
  0.6 23.3 %adjoint_sweeps.1 = (bf16[12,96,256]{2,1,0:T(8,128)(2,1)S(1)}, f32[1,12]{1,0:T(1,128)S(1)}) custom-call(bf16[12,96,256]{2,1,0:T(8,128)(2,1)} %bitcast.13, bf16[96,256]{1,0:T(8,128)(2,1)} %bitcast.16, s32[1,96]{1,0:T(1,128)} %bitcast.18, s32[1,96]{1,0:T(1,128)} %bitcast.19, bf16[12,192,96]{2,1,0:T(8,128)(2,1)} %bitcast.14, bf16[12,5,192,96]{3,2,1,0:T(8,128)(2,1)} %bitcast.12, ...), custom_call_target="tpu_custom_call" | custom-call | tf_op jit(solution)/shard_map/adjoint_sweeps/pallas_call | solution.py:352
  24.0 0.8 %copy.13 = bf16[1,12,96,256]{3,2,1,0:T(8,128)(2,1)} copy(bf16[1,12,96,256]{3,2,1,0:T(8,128)(2,1)S(1)} %bitcast.10) | data formatting | bytes 1179648
  24.8 0.5 %copy.14 = f32[12]{0:T(128)} copy(f32[12]{0:T(128)S(1)} %bitcast.11) | data formatting | bytes 96

commit v4 on v3

--- a/solution.py
+++ b/solution.py
@@ -154,29 +154,22 @@
     idx_recv[me] = idx_send[me]
     pack_recv[me] = pack_send[me]
 
-    loads[3].wait()
-    loads[4].wait()
-
-    @pl.loop(0, nb // 4)
+    for i in (3, 4, 5, 6, 8):
+        loads[i].wait()
+
+    @pl.loop(0, nb // 2)
     def _(g):
-        for i in range(4):
-            b = g * 4 + i
+        for b in (g * 2, g * 2 + 1):
             stiff_resp[b] = dot(stiff[b], resp[b])
-
-    loads[5].wait()
-    loads[6].wait()
-    loads[8].wait()
-
-    @pl.loop(0, nb)
-    def _(b):
-        tiles[b, :, :bs] = diag[b]
-        for k in range(nnb):
-            tiles[b, :, (k + 1) * LANES : (k + 1) * LANES + bs] = off[b, k]
-        for side, column in enumerate((0, nb + 1)):
-            total = jnp.zeros((2 * bs, bs), F32)
+            tiles[b, :, :bs] = diag[b]
             for k in range(nnb):
-                total = total + jnp.where(cols[k, b] == column, 1.0, 0.0) * off[b, k].astype(F32)
-            edge_tiles[b, :, side * LANES : side * LANES + bs] = total.astype(BF16)
+                tiles[b, :, (k + 1) * LANES : (k + 1) * LANES + bs] = off[b, k]
+            for side, column in enumerate((0, nb + 1)):
+                total = jnp.zeros((2 * bs, bs), BF16)
+                for k in range(nnb):
+                    reads = jnp.full((2 * bs, bs), jnp.where(cols[k, b] == column, 1.0, 0.0), F32).astype(BF16)
+                    total = total + reads * off[b, k]
+                edge_tiles[b, :, side * LANES : side * LANES + bs] = total
 
     for j in range(1, n_sub):
         source = lax.rem(me + n_sub - j, n_sub)
@@ -190,10 +183,10 @@
         numbers = numbers + idx_recv[p]
     numbers = jnp.broadcast_to(numbers - 1.0, (bs, lanes))
 
-    @pl.loop(0, nb // 2)
+    @pl.loop(0, nb // 4)
     def _(g):
-        for i in range(2):
-            b = g * 2 + i
+        for i in range(4):
+            b = g * 4 + i
             here = iota((bs, lanes), 0).astype(F32) + (b * bs).astype(F32)
             hit = jnp.where(numbers == here, 1.0, 0.0)
             scat[b] = hit.astype(BF16)
@@ -272,14 +265,12 @@
                 ext[step + 1][b + 1, :bs, :] = value.astype(BF16)
 
     def inner(work):
-        @pl.loop(0, (nb - 2) // group)
-        def _(g):
-            work([1 + g * group + i for i in range(group)])
+        for g in range(0, nb - 2, group):
+            work([1 + g + i for i in range(group)])
 
     def every(work):
-        @pl.loop(0, nb // 4)
-        def _(g):
-            work([g * 4 + i for i in range(4)])
+        for g in range(0, nb, 4):
+            work([g + i for i in range(4)])
 
     first([0, nb - 1])
     halo_start(0)

time: 25.4 us -> 25.1 us (0.988)
  Pallas kernels: 23.3 us -> 23 us
    pallas_call x1, Pallas kernels: 23.3 us -> 23 us  [shards(): pl.pallas_call(functools.partial(kernel, n_sub, n_freq, slots, group), ou...]
where the time goes in v4:
time: 25.1 us; the launch traced here: 25 us
  Pallas kernels  23 us (92%)
  local copies, waits for them, and re-layouts  1.33 us (5%)
  between operations  0.64 us (3%)
    pallas_call x1, Pallas kernels, shards(): pl.pallas_call(functools.partial(kernel, n_sub, n_freq, slots, group), ou...  23 us
    unnamed x2, local copies, waits for them, and re-layouts  1.33 us

profile of v4, /device:TPU:0, one launch (start us, length us, event | category | flops | bytes accessed | tf_op | source)
XLA Modules:
  0.0 25.0 jit_solution(14810068344698146954)
XLA Ops:
  0.6 23.0 %adjoint_sweeps.1 = (bf16[12,96,256]{2,1,0:T(8,128)(2,1)S(1)}, f32[1,12]{1,0:T(1,128)S(1)}) custom-call(bf16[12,96,256]{2,1,0:T(8,128)(2,1)} %bitcast.13, bf16[96,256]{1,0:T(8,128)(2,1)} %bitcast.16, s32[1,96]{1,0:T(1,128)} %bitcast.18, s32[1,96]{1,0:T(1,128)} %bitcast.19, bf16[12,192,96]{2,1,0:T(8,128)(2,1)} %bitcast.14, bf16[12,5,192,96]{3,2,1,0:T(8,128)(2,1)} %bitcast.12, ...), custom_call_target="tpu_custom_call" | custom-call | tf_op jit(solution)/shard_map/adjoint_sweeps/pallas_call | solution.py:343
  23.6 0.8 %copy.13 = bf16[1,12,96,256]{3,2,1,0:T(8,128)(2,1)} copy(bf16[1,12,96,256]{3,2,1,0:T(8,128)(2,1)S(1)} %bitcast.10) | data formatting | bytes 1179648
  24.4 0.5 %copy.14 = f32[12]{0:T(128)} copy(f32[12]{0:T(128)S(1)} %bitcast.11) | data formatting | bytes 96

commit v5 on v4

--- a/solution.py
+++ b/solution.py
@@ -43,7 +43,7 @@
     n_sub, n_freq, slots, group,
     resp_hbm, meas_hbm, owner_hbm, row_hbm, diag_hbm, off_hbm, cols_hbm, prec_hbm, stiff_hbm,
     out, grad,
-    meas, owner, row, cols, resp, diag, off, prec, stiff, tiles, edge_tiles, ext_0, ext_1, hal_0, hal_1, load, rest, lam, stiff_resp, scat,
+    meas, owner, row, cols, resp, diag, off, prec, stiff, tiles, edge_tiles, ext_0, ext_1, hal_0, hal_1, load, rest, lam, upd, stiff_resp, tee, scat,
     idx_send, idx_recv, pack_send, pack_recv, meas_all, part, part_recv,
     in_sem, idx_ss, idx_rs, pack_ss, pack_rs, halo_ss, halo_rs, part_ss, part_rs,
 ):
@@ -154,13 +154,19 @@
     idx_recv[me] = idx_send[me]
     pack_recv[me] = pack_send[me]
 
-    for i in (3, 4, 5, 6, 8):
+    for i in (3, 4, 5, 6, 7, 8):
         loads[i].wait()
 
     @pl.loop(0, nb // 2)
     def _(g):
         for b in (g * 2, g * 2 + 1):
-            stiff_resp[b] = dot(stiff[b], resp[b])
+            value = dot(stiff[b], resp[b])
+            stiff_resp[b] = value
+            turned = jnp.concatenate([value[:, half:], -value[:, :half]], axis=1)
+            tee[b] = lax.dot_general(
+                prec[b], jnp.concatenate([value, turned], axis=0).astype(BF16),
+                (((0,), (0,)), ((), ())), preferred_element_type=F32,
+            )
             tiles[b, :, :bs] = diag[b]
             for k in range(nnb):
                 tiles[b, :, (k + 1) * LANES : (k + 1) * LANES + bs] = off[b, k]
@@ -192,7 +198,6 @@
             scat[b] = hit.astype(BF16)
             load[b] = jnp.sum(hit, axis=1, keepdims=True) * resp[b].astype(F32)
 
-    loads[7].wait()
     for j in range(1, n_sub):
         source = lax.rem(me + n_sub - j, n_sub)
         pltpu.make_async_remote_copy(
@@ -249,20 +254,30 @@
             values.append(load[b] - combine(dot(tiles[b], jnp.concatenate(near, axis=0))))
         for b, value in zip(blocks, values):
             rest[b] = value
+            if step == SWEEPS - 2:
+                terms = jnp.sum(lam[b] * stiff_resp[b], axis=0, keepdims=True)
+                part[b : b + 1, :] = terms[:, :half] + terms[:, half:]
+
+    def updates(step, blocks):
+        beside = hal[step][...].reshape(2 * LANES, width)
+        return [(rest[b] - combine(dot(edge_tiles[b], beside))).astype(BF16) for b in blocks]
 
     def finish(step, blocks):
-        beside = hal[step][...].reshape(2 * LANES, width)
-        updates = [(rest[b] - combine(dot(edge_tiles[b], beside))).astype(BF16) for b in blocks]
-        new = [lam[b] + combine(dot(prec[b], value)) for b, value in zip(blocks, updates)]
-        last = step == SWEEPS - 2
+        values = updates(step, blocks)
+        new = [lam[b] + combine(dot(prec[b], value)) for b, value in zip(blocks, values)]
         for b, value in zip(blocks, new):
-            if last:
-                out[b] = value.astype(BF16)
-                terms = jnp.sum(value * stiff_resp[b], axis=0, keepdims=True)
-                part[pl.ds(b, 1), :] = terms[:, :half] + terms[:, half:]
-            else:
-                lam[b] = value
-                ext[step + 1][b + 1, :bs, :] = value.astype(BF16)
+            lam[b] = value
+            ext[step + 1][b + 1, :bs, :] = value.astype(BF16)
+
+    def last_updates(blocks):
+        for b, value in zip(blocks, updates(SWEEPS - 2, blocks)):
+            upd[b] = value
+            terms = jnp.sum(value.astype(F32) * tee[b], axis=0, keepdims=True)
+            part[b : b + 1, :] += terms[:, :half] + terms[:, half:]
+
+    def last_products(blocks):
+        for b in blocks:
+            out[b] = (lam[b] + combine(dot(prec[b], upd[b]))).astype(BF16)
 
     def inner(work):
         for g in range(0, nb - 2, group):
@@ -283,7 +298,7 @@
             halo_start(step + 1)
             inner(functools.partial(finish, step))
         else:
-            every(functools.partial(finish, step))
+            every(last_updates)
 
     def part_copy(j):
         dest = lax.rem(fr + j, n_freq)
@@ -296,6 +311,7 @@
     for j in range(1, n_freq):
         part_copy(j).start()
     part_recv[fr] = part[...]
+    every(last_products)
     for j in range(1, n_sub):
         idx_copy(j).wait_send()
         pack_copy(j).wait_send()
@@ -323,6 +339,17 @@
     grad[...] = line[:, :nb]
     for j in range(1, n_freq):
         part_copy(j).wait_send()
+
+
+def close(adjoint_in, gradient_in, adjoint, gradient, sems):
+    copies = [
+        pltpu.make_async_copy(adjoint_in, adjoint, sems.at[0]),
+        pltpu.make_async_copy(gradient_in, gradient, sems.at[1]),
+    ]
+    for copy in copies:
+        copy.start()
+    for copy in copies:
+        copy.wait()
 
 
 def shards(
@@ -367,6 +394,8 @@
             pltpu.VMEM((nb, bs, width), F32),
             pltpu.VMEM((nb, bs, width), F32),
             pltpu.VMEM((nb, bs, width), F32),
+            pltpu.VMEM((nb, bs, width), BF16),
+            pltpu.VMEM((nb, bs, width), F32),
             pltpu.VMEM((nb, bs, width), F32),
             pltpu.VMEM((nb, bs, lanes), BF16),
             pltpu.VMEM((n_sub, 1, lanes), F32),
@@ -397,6 +426,17 @@
         precond.reshape(nb, 2 * bs, bs),
         stiff_deriv,
     )))
+    adjoint, gradient = pl.pallas_call(
+        close,
+        out_shape=(
+            jax.ShapeDtypeStruct((nb, bs, width), BF16),
+            jax.ShapeDtypeStruct((1, nb), F32),
+        ),
+        in_specs=[pl.BlockSpec(memory_space=pl.ANY)] * 2,
+        out_specs=(hbm, hbm),
+        scratch_shapes=[dma((2,))],
+        name="results",
+    )(adjoint, gradient)
     return adjoint[None], gradient.reshape(nb)
 
 

time: 25.1 us -> 43.6 us (1.74)
  Pallas kernels: 23 us -> 41.4 us
    pallas_call x0 -> x1, Pallas kernels: none -> 19 us  [shards(): pl.pallas_call(close, out_shape=(jax.ShapeDtypeStruct((nb, bs, width), BF...]
    pallas_call x1, Pallas kernels: 23 us -> 22.4 us  [shards(): pl.pallas_call(functools.partial(kernel, n_sub, n_freq, slots, group), ou...]
    unnamed x2 -> x4, local copies, waits for them, and re-layouts: 1.33 us -> 1.33 us
where the time goes in v5:
time: 43.6 us; the launch traced here: 43.4 us
  Pallas kernels  41.4 us (95%)
  local copies, waits for them, and re-layouts  1.33 us (3%)
  between operations  0.65 us (1%)
    pallas_call x1, Pallas kernels, shards(): pl.pallas_call(functools.partial(kernel, n_sub, n_freq, slots, group), ou...  22.4 us
    pallas_call x1, Pallas kernels, shards(): pl.pallas_call(close, out_shape=(jax.ShapeDtypeStruct((nb, bs, width), BF...  19 us
    unnamed x4, local copies, waits for them, and re-layouts  1.33 us

profile of v5, /device:TPU:0, one launch (start us, length us, event | category | flops | bytes accessed | tf_op | source)
XLA Modules:
  0.0 43.4 jit_solution(14432513508161979953)
XLA Ops:
  0.6 22.4 %adjoint_sweeps.1 = (bf16[12,96,256]{2,1,0:T(8,128)(2,1)S(1)}, f32[1,12]{1,0:T(1,128)S(1)}) custom-call(bf16[12,96,256]{2,1,0:T(8,128)(2,1)} %bitcast.11, bf16[96,256]{1,0:T(8,128)(2,1)} %bitcast.14, s32[1,96]{1,0:T(1,128)} %bitcast.16, s32[1,96]{1,0:T(1,128)} %bitcast.17, bf16[12,192,96]{2,1,0:T(8,128)(2,1)} %bitcast.12, bf16[12,5,192,96]{3,2,1,0:T(8,128)(2,1)} %bitcast.10, ...), custom_call_target="tpu_custom_call" | custom-call | tf_op jit(solution)/shard_map/adjoint_sweeps/pallas_call | solution.py:370
  23.1 0.0 copy-start
  23.1 0.8 %copy-done = bf16[12,96,256]{2,1,0:T(8,128)(2,1)} copy-done((bf16[12,96,256]{2,1,0:T(8,128)(2,1)}, bf16[12,96,256]{2,1,0:T(8,128)(2,1)S(1)}, u32[]{:S(2)}) %copy-start) | copy-done | bytes 589848
  23.9 0.0 copy-start.1
  23.9 0.5 %copy-done.1 = f32[1,12]{1,0:T(1,128)} copy-done((f32[1,12]{1,0:T(1,128)}, f32[1,12]{1,0:T(1,128)S(1)}, u32[]{:S(2)}) %copy-start.1) | copy-done | bytes 72
  24.4 19.0 %results.1 = (bf16[12,96,256]{2,1,0:T(8,128)(2,1)}, f32[1,12]{1,0:T(1,128)}) custom-call(bf16[12,96,256]{2,1,0:T(8,128)(2,1)} %copy-done, f32[1,12]{1,0:T(1,128)} %copy-done.1), custom_call_target="tpu_custom_call" | custom-call | tf_op jit(solution)/shard_map/results/pallas_call | solution.py:429
Async XLA Ops:
  23.1 0.8 %copy-start = (bf16[12,96,256]{2,1,0:T(8,128)(2,1)}, bf16[12,96,256]{2,1,0:T(8,128)(2,1)S(1)}, u32[]{:S(2)}) copy-start(bf16[12,96,256]{2,1,0:T(8,128)(2,1)S(1)} %get-tuple-element.6.adjoint_in) | copy-start | bytes 1769476
  23.9 0.5 %copy-start.1 = (f32[1,12]{1,0:T(1,128)}, f32[1,12]{1,0:T(1,128)S(1)}, u32[]{:S(2)}) copy-start(f32[1,12]{1,0:T(1,128)S(1)} %get-tuple-element.7.gradient_in) | copy-start | bytes 148

commit v6 on v5

--- a/solution.py
+++ b/solution.py
@@ -198,16 +198,20 @@
             scat[b] = hit.astype(BF16)
             load[b] = jnp.sum(hit, axis=1, keepdims=True) * resp[b].astype(F32)
 
-    for j in range(1, n_sub):
+    def place_rows(source):
+        rows = pack_recv[source].astype(F32)
+        spot = pl.multiple_of(source * slots, 8)
+        meas_all[pl.ds(spot, slots), :] = jnp.concatenate([rows[:slots], rows[slots:]], axis=1)
+
+    place_rows(me)
+    for j in reversed(far_first):
         source = lax.rem(me + n_sub - j, n_sub)
         pltpu.make_async_remote_copy(
             src_ref=pack_send.at[source], dst_ref=pack_recv.at[source],
             send_sem=pack_ss.at[source], recv_sem=pack_rs.at[source],
             device_id={"sub": source}, device_id_type=MESH,
         ).wait_recv()
-    for p in range(n_sub):
-        rows = pack_recv[p].astype(F32)
-        meas_all[p * slots : (p + 1) * slots, :] = jnp.concatenate([rows[:slots], rows[slots:]], axis=1)
+        place_rows(source)
     rows_in = meas_all[...].astype(BF16)
 
     def halo(step, low):
@@ -279,22 +283,26 @@
         for b in blocks:
             out[b] = (lam[b] + combine(dot(prec[b], upd[b]))).astype(BF16)
 
+    def edges(work):
+        work([0, nb - 1])
+        work([1 + i for i in range(group)])
+
     def inner(work):
-        for g in range(0, nb - 2, group):
+        for g in range(group, nb - 2, group):
             work([1 + g + i for i in range(group)])
 
     def every(work):
         for g in range(0, nb, 4):
             work([g + i for i in range(4)])
 
-    first([0, nb - 1])
+    edges(first)
     halo_start(0)
     inner(first)
     for step in range(SWEEPS - 1):
         every(functools.partial(interior, step))
         halo_wait(step)
         if step < SWEEPS - 2:
-            finish(step, [0, nb - 1])
+            edges(functools.partial(finish, step))
             halo_start(step + 1)
             inner(functools.partial(finish, step))
         else:
@@ -432,7 +440,7 @@
             jax.ShapeDtypeStruct((nb, bs, width), BF16),
             jax.ShapeDtypeStruct((1, nb), F32),
         ),
-        in_specs=[pl.BlockSpec(memory_space=pl.ANY)] * 2,
+        in_specs=[vmem, vmem],
         out_specs=(hbm, hbm),
         scratch_shapes=[dma((2,))],
         name="results",

time: 43.6 us -> 27.2 us (0.62)
  Pallas kernels: 41.4 us -> 25.1 us
    pallas_call x1, Pallas kernels: 19 us -> 1.9 us  [shards(): pl.pallas_call(close, out_shape=(jax.ShapeDtypeStruct((nb, bs, width), BF...]
    pallas_call x1, Pallas kernels: 22.4 us -> 23.2 us  [shards(): pl.pallas_call(functools.partial(kernel, n_sub, n_freq, slots, group), ou...]
where the time goes in v6:
time: 27.2 us; the launch traced here: 27.1 us
  Pallas kernels  25.1 us (92%)
  local copies, waits for them, and re-layouts  1.33 us (5%)
  between operations  0.65 us (2%)
    pallas_call x1, Pallas kernels, shards(): pl.pallas_call(functools.partial(kernel, n_sub, n_freq, slots, group), ou...  23.2 us
    pallas_call x1, Pallas kernels, shards(): pl.pallas_call(close, out_shape=(jax.ShapeDtypeStruct((nb, bs, width), BF...  1.9 us
    unnamed x4, local copies, waits for them, and re-layouts  1.33 us

profile of v6, /device:TPU:0, one launch (start us, length us, event | category | flops | bytes accessed | tf_op | source)
XLA Modules:
  0.0 27.1 jit_solution(1824139921491002435)
XLA Ops:
  0.6 23.2 %adjoint_sweeps.1 = (bf16[12,96,256]{2,1,0:T(8,128)(2,1)S(1)}, f32[1,12]{1,0:T(1,128)S(1)}) custom-call(bf16[12,96,256]{2,1,0:T(8,128)(2,1)} %bitcast.11, bf16[96,256]{1,0:T(8,128)(2,1)} %bitcast.14, s32[1,96]{1,0:T(1,128)} %bitcast.16, s32[1,96]{1,0:T(1,128)} %bitcast.17, bf16[12,192,96]{2,1,0:T(8,128)(2,1)} %bitcast.12, bf16[12,5,192,96]{3,2,1,0:T(8,128)(2,1)} %bitcast.10, ...), custom_call_target="tpu_custom_call" | custom-call | tf_op jit(solution)/shard_map/adjoint_sweeps/pallas_call | solution.py:378
  23.8 0.0 copy-start
  23.8 0.8 %copy-done = bf16[12,96,256]{2,1,0:T(8,128)(2,1)} copy-done((bf16[12,96,256]{2,1,0:T(8,128)(2,1)}, bf16[12,96,256]{2,1,0:T(8,128)(2,1)S(1)}, u32[]{:S(2)}) %copy-start) | copy-done | bytes 589848
  24.6 0.0 copy-start.1
  24.6 0.5 %copy-done.1 = f32[1,12]{1,0:T(1,128)} copy-done((f32[1,12]{1,0:T(1,128)}, f32[1,12]{1,0:T(1,128)S(1)}, u32[]{:S(2)}) %copy-start.1) | copy-done | bytes 72
  25.2 1.9 %results.1 = (bf16[12,96,256]{2,1,0:T(8,128)(2,1)}, f32[1,12]{1,0:T(1,128)}) custom-call(bf16[12,96,256]{2,1,0:T(8,128)(2,1)} %copy-done, f32[1,12]{1,0:T(1,128)} %copy-done.1), custom_call_target="tpu_custom_call" | custom-call | tf_op jit(solution)/shard_map/results/pallas_call | solution.py:437
Async XLA Ops:
  23.8 0.8 %copy-start = (bf16[12,96,256]{2,1,0:T(8,128)(2,1)}, bf16[12,96,256]{2,1,0:T(8,128)(2,1)S(1)}, u32[]{:S(2)}) copy-start(bf16[12,96,256]{2,1,0:T(8,128)(2,1)S(1)} %get-tuple-element.6.adjoint_in) | copy-start | bytes 1769476
  24.6 0.5 %copy-start.1 = (f32[1,12]{1,0:T(1,128)}, f32[1,12]{1,0:T(1,128)S(1)}, u32[]{:S(2)}) copy-start(f32[1,12]{1,0:T(1,128)S(1)} %get-tuple-element.7.gradient_in) | copy-start | bytes 148

commit v7 on v5

--- a/solution.py
+++ b/solution.py
@@ -339,17 +339,6 @@
     grad[...] = line[:, :nb]
     for j in range(1, n_freq):
         part_copy(j).wait_send()
-
-
-def close(adjoint_in, gradient_in, adjoint, gradient, sems):
-    copies = [
-        pltpu.make_async_copy(adjoint_in, adjoint, sems.at[0]),
-        pltpu.make_async_copy(gradient_in, gradient, sems.at[1]),
-    ]
-    for copy in copies:
-        copy.start()
-    for copy in copies:
-        copy.wait()
 
 
 def shards(
@@ -426,17 +415,6 @@
         precond.reshape(nb, 2 * bs, bs),
         stiff_deriv,
     )))
-    adjoint, gradient = pl.pallas_call(
-        close,
-        out_shape=(
-            jax.ShapeDtypeStruct((nb, bs, width), BF16),
-            jax.ShapeDtypeStruct((1, nb), F32),
-        ),
-        in_specs=[pl.BlockSpec(memory_space=pl.ANY)] * 2,
-        out_specs=(hbm, hbm),
-        scratch_shapes=[dma((2,))],
-        name="results",
-    )(adjoint, gradient)
     return adjoint[None], gradient.reshape(nb)
 
 

time: 43.6 us -> 24.5 us (0.56)
  Pallas kernels: 41.4 us -> 22.4 us
    pallas_call x1 -> x0, Pallas kernels: 19 us -> none  [shards(): pl.pallas_call(close, out_shape=(jax.ShapeDtypeStruct((nb, bs, width), BF...]
    unnamed x4 -> x2, local copies, waits for them, and re-layouts: 1.33 us -> 1.33 us
where the time goes in v7:
time: 24.5 us; the launch traced here: 24.4 us
  Pallas kernels  22.4 us (91%)
  local copies, waits for them, and re-layouts  1.33 us (5%)
  between operations  0.64 us (3%)
    pallas_call x1, Pallas kernels, shards(): pl.pallas_call(functools.partial(kernel, n_sub, n_freq, slots, group), ou...  22.4 us
    unnamed x2, local copies, waits for them, and re-layouts  1.33 us

profile of v7, /device:TPU:0, one launch (start us, length us, event | category | flops | bytes accessed | tf_op | source)
XLA Modules:
  0.0 24.4 jit_solution(16292205689142077480)
XLA Ops:
  0.6 22.4 %adjoint_sweeps.1 = (bf16[12,96,256]{2,1,0:T(8,128)(2,1)S(1)}, f32[1,12]{1,0:T(1,128)S(1)}) custom-call(bf16[12,96,256]{2,1,0:T(8,128)(2,1)} %bitcast.13, bf16[96,256]{1,0:T(8,128)(2,1)} %bitcast.16, s32[1,96]{1,0:T(1,128)} %bitcast.18, s32[1,96]{1,0:T(1,128)} %bitcast.19, bf16[12,192,96]{2,1,0:T(8,128)(2,1)} %bitcast.14, bf16[12,5,192,96]{3,2,1,0:T(8,128)(2,1)} %bitcast.12, ...), custom_call_target="tpu_custom_call" | custom-call | tf_op jit(solution)/shard_map/adjoint_sweeps/pallas_call | solution.py:359
  23.1 0.8 %copy.13 = bf16[1,12,96,256]{3,2,1,0:T(8,128)(2,1)} copy(bf16[1,12,96,256]{3,2,1,0:T(8,128)(2,1)S(1)} %bitcast.10) | data formatting | bytes 1179648
  23.9 0.5 %copy.14 = f32[12]{0:T(128)} copy(f32[12]{0:T(128)S(1)} %bitcast.11) | data formatting | bytes 96
